TPU v7x, 32 devices: a whole 2x2x4 slice. The times are simulated.
32 devices in a mesh: rep: 4 (over z), dp: 8 (over y, x, core).
Axes of the slice: x: 2, y: 2, z: 4, core: 2. Of those that a mesh axis runs over, the one named last changes fastest.
Arguments:
- decoder_input: bfloat16 [32768, 512], P(('rep', 'dp')), may hold values from -20 to 20
- target_embedding: bfloat16 [32768, 512], P(('rep', 'dp')), may hold values from -20 to 20
- encoder_states: bfloat16 [32768, 512], P(('rep', 'dp')), may hold values from -20 to 20
- cotangent: float32 [32768, 512], P(('rep', 'dp')), may hold values from -6 to 6
- segments: int32 [32, 1024], P(('rep', 'dp')), may hold values from -1 to 50, as said below
- hamming: int32 [32, 51], P(('rep', 'dp')), may hold values from 0 to 63
- priority: int32 [32, 1024], P(('rep', 'dp')), may hold values from 0 to 1023
- attention_weight: float32 [8, 512, 512], P(None, 'dp')
- attention_first: float32 [8, 512, 512], P(None, 'dp')
- attention_second: float32 [8, 512, 512], P(None, 'dp'), as said below
- expand_weight: float32 [512, 2048], P('dp'), may hold values from -0.25 to 0.25
- expand_first: float32 [512, 2048], P('dp')
- expand_second: float32 [512, 2048], P('dp'), as said below
- contract_weight: float32 [2048, 512], P('dp'), may hold values from -0.125 to 0.125
- contract_first: float32 [2048, 512], P('dp')
- contract_second: float32 [2048, 512], P('dp'), as said below
- vector_weight: float32 [17, 512], P(None, 'dp')
- vector_first: float32 [17, 512], P(None, 'dp')
- vector_second: float32 [17, 512], P(None, 'dp'), as said below
Outputs:
- layer_output: bfloat16 [32768, 512], P(('rep', 'dp'))
- input_grad: float32 [32768, 512], P(('rep', 'dp'))
- encoder_grad: float32 [32768, 512], P(('rep', 'dp'))
- attention_grad: float32 [8, 512, 512], P(None, 'dp')
- attention_first_new: float32 [8, 512, 512], P(None, 'dp')
- attention_second_new: float32 [8, 512, 512], P(None, 'dp')
- attention_weight_new: float32 [8, 512, 512], P(None, 'dp')
- expand_grad: float32 [512, 2048], P('dp')
- expand_first_new: float32 [512, 2048], P('dp')
- expand_second_new: float32 [512, 2048], P('dp')
- expand_weight_new: float32 [512, 2048], P('dp')
- contract_grad: float32 [2048, 512], P('dp')
- contract_first_new: float32 [2048, 512], P('dp')
- contract_second_new: float32 [2048, 512], P('dp')
- contract_weight_new: float32 [2048, 512], P('dp')
- vector_grad: float32 [17, 512], P(None, 'dp')
- vector_first_new: float32 [17, 512], P(None, 'dp')
- vector_second_new: float32 [17, 512], P(None, 'dp')
- vector_weight_new: float32 [17, 512], P(None, 'dp')
- grad_norm: float32 [], replicated
Inputs may be any that keep to these rules, and one draw needn't show every extreme that they name: `segments`: in each row, ids start at 0, never fall, each id is one run of positions, and padding (-1) stands only at the row's end. `attention_second`: Positive. `expand_second`: Positive. `contract_second`: Positive. `vector_second`: Positive.
All inputs are finite; a program needn't handle non-finite values.
Results may differ from a plain program's by a relative error of at most 0.023.
The roundings to bfloat16 on the way count: a program that leaves them out, or rounds other values in their place, can miss the bound.
Values may be sent and summed in bfloat16 or wider, within the bound.
A program may use at most 256 MiB of HBM per device.

v0:
```python
import math

import jax
import jax.numpy as jnp
from jax import lax
from jax.sharding import PartitionSpec as P

H = 8
STEP = 10


NORM_EPS = 1e-05
CLIP_NORM = 1.0
BETA_ONE = 0.9
BETA_TWO = 0.999
ADAM_EPS = 1e-08
WEIGHT_DECAY = 0.01
RATE_MATRIX = 0.03
RATE_VECTOR = 0.5
NEG_FILL = -1000000000.0


def layer_norm(values, gain, shift):
    center = jnp.mean(values, axis=-1, keepdims=True)
    centred = values - center
    spread = jnp.mean(centred * centred, axis=-1, keepdims=True)
    return centred * lax.rsqrt(spread + NORM_EPS) * gain + shift


def glance(segments, hamming, priority, slot_count):
    row_len = segments.shape[1]
    slot_ids = lax.broadcasted_iota(jnp.int32, (1, 1, slot_count), 2)
    member = (segments[:, :, None] == slot_ids).astype(jnp.int32)
    counts = jnp.sum(member, axis=1, keepdims=True)
    seg_length = jnp.sum(member * counts, axis=2)
    distance = jnp.sum(member * hamming[:, None, :], axis=2)
    return 2 * priority * seg_length < distance * row_len


def project(inputs, matrix):
    return jnp.dot(inputs, matrix, preferred_element_type=jnp.float32)


def back_project(grads, matrix):
    return lax.dot_general(
        grads, matrix, (((1,), (1,)), ((), ())), preferred_element_type=jnp.float32
    )


def outer_sum(left, right):
    return lax.dot_general(
        left, right, (((0,), (0,)), ((), ())), preferred_element_type=jnp.float32
    )


def column_sum(grads):
    return jnp.sum(grads, axis=0, dtype=jnp.float32)


def block_scores(query_block, key_rows, query_seg, key_seg, scale):
    scores = (
        jnp.einsum("qhd,khd->hqk", query_block, key_rows, preferred_element_type=jnp.float32)
        * scale
    )
    same = query_seg[None, :, None] == key_seg[None, None, :]
    return jnp.where(same, scores, NEG_FILL)


def attend_row(query_rows, key_rows, value_rows, segment_row):
    length = query_rows.shape[0]
    block_len = min(512, length)
    scale = 1.0 / math.sqrt(query_rows.shape[2])
    mixed_parts = []
    total_parts = []
    for offset in range(0, length, block_len):
        query_block = query_rows[offset : offset + block_len]
        scores = block_scores(
            query_block, key_rows, segment_row[offset : offset + block_len], segment_row, scale
        )
        highest = jnp.max(scores, axis=2, keepdims=True)
        raised = jnp.exp(scores - highest)
        totals = jnp.sum(raised, axis=2, keepdims=True)
        shares = (raised / totals).astype(jnp.bfloat16)
        mixed = jnp.einsum("hqk,khd->qhd", shares, value_rows, preferred_element_type=jnp.float32)
        mixed_parts.append(mixed.reshape(block_len, -1).astype(jnp.bfloat16))
        total_parts.append(highest[:, :, 0] + jnp.log(totals[:, :, 0]))
    return (jnp.concatenate(mixed_parts, axis=0), jnp.concatenate(total_parts, axis=1))


def attend_back(query_rows, key_rows, value_rows, segment_row, log_total, grad_rows):
    length = query_rows.shape[0]
    block_len = min(512, length)
    scale = 1.0 / math.sqrt(query_rows.shape[2])
    key_grad = jnp.zeros(key_rows.shape, jnp.float32)
    value_grad = jnp.zeros(value_rows.shape, jnp.float32)
    query_parts = []
    for offset in range(0, length, block_len):
        query_block = query_rows[offset : offset + block_len]
        grad_block = grad_rows[offset : offset + block_len]
        scores = block_scores(
            query_block, key_rows, segment_row[offset : offset + block_len], segment_row, scale
        )
        shares = jnp.exp(scores - log_total[:, offset : offset + block_len, None])
        share_grad = jnp.einsum(
            "qhd,khd->hqk", grad_block, value_rows, preferred_element_type=jnp.float32
        )
        inner = jnp.sum(shares * share_grad, axis=2, keepdims=True)
        score_grad = (shares * (share_grad - inner)).astype(jnp.bfloat16)
        query_parts.append(
            jnp.einsum("hqk,khd->qhd", score_grad, key_rows, preferred_element_type=jnp.float32)
            * scale
        )
        key_grad = (
            key_grad
            + jnp.einsum(
                "hqk,qhd->khd", score_grad, query_block, preferred_element_type=jnp.float32
            )
            * scale
        )
        value_grad = value_grad + jnp.einsum(
            "hqk,qhd->khd",
            shares.astype(jnp.bfloat16),
            grad_block,
            preferred_element_type=jnp.float32,
        )
    return (jnp.concatenate(query_parts, axis=0), key_grad, value_grad)


def run_attention(query_low, key_low, value_low, segments, heads):
    row_count, row_len = segments.shape

    def shaped(matrix):
        return matrix.reshape(row_count, row_len, heads, -1)

    def one_row(packed):
        return attend_row(packed[0], packed[1], packed[2], packed[3])

    mixed, log_total = lax.map(
        one_row, (shaped(query_low), shaped(key_low), shaped(value_low), segments)
    )
    return (mixed.reshape(row_count * row_len, -1), log_total)


def run_backward(query_low, key_low, value_low, log_total, mixed_grad, segments, heads):
    row_count, row_len = segments.shape

    def shaped(matrix):
        return matrix.reshape(row_count, row_len, heads, -1)

    def one_row(packed):
        return attend_back(packed[0], packed[1], packed[2], packed[3], packed[4], packed[5])

    query_grad, key_grad, value_grad = lax.map(
        one_row,
        (
            shaped(query_low),
            shaped(key_low),
            shaped(value_low),
            segments,
            log_total,
            shaped(mixed_grad),
        ),
    )
    flat = row_count * row_len
    return (
        query_grad.reshape(flat, -1).astype(jnp.bfloat16),
        key_grad.reshape(flat, -1).astype(jnp.bfloat16),
        value_grad.reshape(flat, -1).astype(jnp.bfloat16),
    )


def adamw_update(grad, weight, first, second, factor, rate):
    clipped = grad * factor
    first_new = BETA_ONE * first + (1.0 - BETA_ONE) * clipped
    second_new = BETA_TWO * second + (1.0 - BETA_TWO) * clipped * clipped
    first_hat = first_new / (1.0 - BETA_ONE**STEP)
    second_hat = second_new / (1.0 - BETA_TWO**STEP)
    weight_new = weight - rate * (
        first_hat / (jnp.sqrt(second_hat) + ADAM_EPS) + WEIGHT_DECAY * weight
    )
    return (clipped, first_new, second_new, weight_new)


def per_device(
    decoder_input,
    target_embedding,
    encoder_states,
    cotangent,
    segments,
    hamming,
    priority,
    attention_weight,
    attention_first,
    attention_second,
    expand_weight,
    expand_first,
    expand_second,
    contract_weight,
    contract_first,
    contract_second,
    vector_weight,
    vector_first,
    vector_second,
):
    heads = H
    attention_all, expand_all, contract_all, vector_low = (
        lax.all_gather(attention_weight.astype(jnp.bfloat16), "dp", axis=1, tiled=True),
        lax.all_gather(expand_weight.astype(jnp.bfloat16), "dp", axis=0, tiled=True),
        lax.all_gather(contract_weight.astype(jnp.bfloat16), "dp", axis=0, tiled=True),
        lax.all_gather(vector_weight.astype(jnp.bfloat16), "dp", axis=1, tiled=True),
    )
    vectors = vector_low.astype(jnp.float32)
    hidden_width = expand_all.shape[1]
    hidden_bias = vectors[13:].reshape(hidden_width)
    glanced = glance(segments, hamming, priority, hamming.shape[1]).reshape(-1)
    layer_input = jnp.where(glanced[:, None], target_embedding, decoder_input)
    input_float = layer_input.astype(jnp.float32)
    valid_mask = (segments >= 0).reshape(-1).astype(jnp.float32)
    query_self = (project(layer_input, attention_all[0]) + vectors[6]).astype(jnp.bfloat16)
    key_self = project(layer_input, attention_all[1]).astype(jnp.bfloat16)
    value_self = (project(layer_input, attention_all[2]) + vectors[7]).astype(jnp.bfloat16)
    mixed_self, total_self = run_attention(query_self, key_self, value_self, segments, heads)
    first_sum = input_float + project(mixed_self, attention_all[3]) + vectors[8]
    first_norm, first_pull = jax.vjp(layer_norm, first_sum, vectors[0], vectors[1])
    first_low = first_norm.astype(jnp.bfloat16)
    query_cross = (project(first_low, attention_all[4]) + vectors[9]).astype(jnp.bfloat16)
    key_cross = project(encoder_states, attention_all[5]).astype(jnp.bfloat16)
    value_cross = (project(encoder_states, attention_all[6]) + vectors[10]).astype(jnp.bfloat16)
    mixed_cross, total_cross = run_attention(query_cross, key_cross, value_cross, segments, heads)
    second_sum = first_norm + project(mixed_cross, attention_all[7]) + vectors[11]
    second_norm, second_pull = jax.vjp(layer_norm, second_sum, vectors[2], vectors[3])
    second_low = second_norm.astype(jnp.bfloat16)
    expanded = project(second_low, expand_all) + hidden_bias
    activated = jax.nn.gelu(expanded).astype(jnp.bfloat16)
    third_sum = second_norm + project(activated, contract_all) + vectors[12]
    result, third_pull = jax.vjp(layer_norm, third_sum, vectors[4], vectors[5])
    layer_output = result.astype(jnp.bfloat16)
    third_grad, gain_three, shift_three = third_pull(cotangent * valid_mask[:, None])
    branch_grad = third_grad.astype(jnp.bfloat16)
    bias_contract = column_sum(branch_grad)
    contract_raw = outer_sum(activated, branch_grad)
    activated_grad = back_project(branch_grad, contract_all)
    gelu_pull = jax.vjp(jax.nn.gelu, expanded)[1]
    expanded_grad = gelu_pull(activated_grad)[0].astype(jnp.bfloat16)
    bias_expand = column_sum(expanded_grad)
    expand_raw = outer_sum(second_low, expanded_grad)
    second_norm_grad = third_grad + back_project(expanded_grad, expand_all)
    second_grad, gain_two, shift_two = second_pull(second_norm_grad)
    cross_grad = second_grad.astype(jnp.bfloat16)
    bias_cross_out = column_sum(cross_grad)
    weight_cross_out = outer_sum(mixed_cross, cross_grad)
    mixed_cross_grad = back_project(cross_grad, attention_all[7]).astype(jnp.bfloat16)
    query_cross_grad, key_cross_grad, value_cross_grad = run_backward(
        query_cross, key_cross, value_cross, total_cross, mixed_cross_grad, segments, heads
    )
    bias_cross_query = column_sum(query_cross_grad)
    bias_cross_value = column_sum(value_cross_grad)
    weight_cross_query = outer_sum(first_low, query_cross_grad)
    weight_cross_key = outer_sum(encoder_states, key_cross_grad)
    weight_cross_value = outer_sum(encoder_states, value_cross_grad)
    encoder_grad = back_project(key_cross_grad, attention_all[5]) + back_project(
        value_cross_grad, attention_all[6]
    )
    first_norm_grad = second_grad + back_project(query_cross_grad, attention_all[4])
    first_grad, gain_one, shift_one = first_pull(first_norm_grad)
    self_grad = first_grad.astype(jnp.bfloat16)
    bias_self_out = column_sum(self_grad)
    weight_self_out = outer_sum(mixed_self, self_grad)
    mixed_self_grad = back_project(self_grad, attention_all[3]).astype(jnp.bfloat16)
    query_self_grad, key_self_grad, value_self_grad = run_backward(
        query_self, key_self, value_self, total_self, mixed_self_grad, segments, heads
    )
    bias_self_query = column_sum(query_self_grad)
    bias_self_value = column_sum(value_self_grad)
    weight_self_query = outer_sum(layer_input, query_self_grad)
    weight_self_key = outer_sum(layer_input, key_self_grad)
    weight_self_value = outer_sum(layer_input, value_self_grad)
    input_grad = (
        first_grad
        + back_project(query_self_grad, attention_all[0])
        + back_project(key_self_grad, attention_all[1])
        + back_project(value_self_grad, attention_all[2])
    )
    attention_raw = jnp.stack(
        [
            weight_self_query,
            weight_self_key,
            weight_self_value,
            weight_self_out,
            weight_cross_query,
            weight_cross_key,
            weight_cross_value,
            weight_cross_out,
        ]
    )
    model_width = vectors.shape[1]
    vector_raw = jnp.concatenate(
        [
            jnp.stack(
                [
                    gain_one,
                    shift_one,
                    gain_two,
                    shift_two,
                    gain_three,
                    shift_three,
                    bias_self_query,
                    bias_self_value,
                    bias_self_out,
                    bias_cross_query,
                    bias_cross_value,
                    bias_cross_out,
                    bias_contract,
                ]
            ),
            bias_expand.reshape(hidden_width // model_width, model_width),
        ],
        axis=0,
    )
    summed = (
        lax.psum(attention_raw.astype(jnp.bfloat16), "rep").astype(jnp.float32),
        lax.psum(expand_raw.astype(jnp.bfloat16), "rep").astype(jnp.float32),
        lax.psum(contract_raw.astype(jnp.bfloat16), "rep").astype(jnp.float32),
        lax.psum(vector_raw.astype(jnp.bfloat16), "rep").astype(jnp.float32),
    )
    shard_grads = (
        lax.psum_scatter(
            summed[0].astype(jnp.bfloat16), "dp", scatter_dimension=1, tiled=True
        ).astype(jnp.float32),
        lax.psum_scatter(
            summed[1].astype(jnp.bfloat16), "dp", scatter_dimension=0, tiled=True
        ).astype(jnp.float32),
        lax.psum_scatter(
            summed[2].astype(jnp.bfloat16), "dp", scatter_dimension=0, tiled=True
        ).astype(jnp.float32),
        lax.psum_scatter(
            summed[3].astype(jnp.bfloat16), "dp", scatter_dimension=1, tiled=True
        ).astype(jnp.float32),
    )
    attention_shard, expand_shard, contract_shard, vector_shard = shard_grads
    local_square = (
        jnp.sum(attention_shard * attention_shard)
        + jnp.sum(expand_shard * expand_shard)
        + jnp.sum(contract_shard * contract_shard)
        + jnp.sum(vector_shard * vector_shard)
    )
    total_square = lax.psum(local_square, "dp")
    grad_norm = jnp.sqrt(total_square)
    factor = CLIP_NORM / jnp.maximum(grad_norm, CLIP_NORM)
    attention_out = adamw_update(
        attention_shard, attention_weight, attention_first, attention_second, factor, RATE_MATRIX
    )
    expand_out = adamw_update(
        expand_shard, expand_weight, expand_first, expand_second, factor, RATE_MATRIX
    )
    contract_out = adamw_update(
        contract_shard, contract_weight, contract_first, contract_second, factor, RATE_MATRIX
    )
    vector_out = adamw_update(
        vector_shard, vector_weight, vector_first, vector_second, factor, RATE_VECTOR
    )
    return (
        layer_output,
        input_grad,
        encoder_grad,
        attention_out[0],
        attention_out[1],
        attention_out[2],
        attention_out[3],
        expand_out[0],
        expand_out[1],
        expand_out[2],
        expand_out[3],
        contract_out[0],
        contract_out[1],
        contract_out[2],
        contract_out[3],
        vector_out[0],
        vector_out[1],
        vector_out[2],
        vector_out[3],
        grad_norm,
    )


def solution(mesh):
    placed = (
        P(("rep", "dp"), None),
        P(("rep", "dp"), None),
        P(("rep", "dp"), None),
        P(("rep", "dp"), None),
        P(("rep", "dp"), None),
        P(("rep", "dp"), None),
        P(("rep", "dp"), None),
        P(None, "dp", None),
        P(None, "dp", None),
        P(None, "dp", None),
        P("dp", None),
        P("dp", None),
        P("dp", None),
        P("dp", None),
        P("dp", None),
        P("dp", None),
        P(None, "dp"),
        P(None, "dp"),
        P(None, "dp"),
    )
    return jax.shard_map(
        per_device,
        mesh=mesh,
        in_specs=placed,
        out_specs=(
            P(("rep", "dp"), None),
            P(("rep", "dp"), None),
            P(("rep", "dp"), None),
            P(None, "dp", None),
            P(None, "dp", None),
            P(None, "dp", None),
            P(None, "dp", None),
            P("dp", None),
            P("dp", None),
            P("dp", None),
            P("dp", None),
            P("dp", None),
            P("dp", None),
            P("dp", None),
            P("dp", None),
            P(None, "dp"),
            P(None, "dp"),
            P(None, "dp"),
            P(None, "dp"),
            P(),
        ),
        check_vma=False,
    )
```

profile of v0, /device:TPU:0, one launch (start us, length us, event | category | flops | bytes accessed | tf_op | source)
XLA Modules:
  0.0 583.8 jit_solution(14004429684474602055)
XLA Ops:
  13.9 10.6 %all-gather = bf16[8,64,17]{1,2,0:T(8,128)(2,1)S(1)} all-gather(bf16[1,64,17]{1,2,0:T(8,128)(2,1)S(1)} %convert_bitcast_fusion), channel_id=1, replica_groups=mesh['rep'=4,'dp'=8] {'dp'}, dimensions={0}, use_global_device_ids=true | all-gather | bytes 19584 | tf_op jit(solution)/shard_map/all_gather | solution.py:210
  35.8 14.3 %all-gather.5.cloned.1.call-done = bf16[8,512,512]{2,1,0:T(8,128)(2,1)} async-done(((bf16[8,64,512]{2,1,0:T(8,128)(2,1)}), bf16[8,512,512]{2,1,0:T(8,128)(2,1)}) %all-gather.5.cloned.1.call-update) | async-done | bytes 4194320 | tf_op jit(solution)/shard_map/all_gather | solution.py:207
  54.6 3.2 fusion.110
  57.8 3.5 fusion.1
  63.8 4.5 fusion.43
  68.3 3.2 fusion.111
  71.5 3.7 fusion
  77.3 3.8 fusion.44
  88.2 7.4 %fusion.113 = (f32[8,512]{1,0:T(8,128)S(1)}, f32[8,512,1024]{2,1,0:T(8,128)}) fusion(bf16[512,8,64]{0,2,1:T(8,128)(2,1)S(1)} %bitcast.254, bf16[1024,8,64]{0,2,1:T(8,128)(2,1)S(1)} %bitcast.246, pred[512,1024]{1,0:T(8,128)(4,1)S(1)} %copy-done.45), kind=kOutput, calls=%fused_computation.239 | convolution fusion | flops 549449728 | bytes 18890752 | tf_op jit(solution)/shard_map/while/body/eval_jaxpr/qhd,khd->hqk/dot_general | solution.py:62
  95.6 3.2 fusion.114
  98.8 13.6 %fusion.3 = f32[8,512]{1,0:T(8,128)S(1)} fusion(f32[8,512,1024]{2,1,0:T(8,128)} %get-tuple-element.301, f32[8,512]{1,0:T(8,128)S(1)} %get-tuple-element.300), kind=kLoop, calls=%fused_computation.27 | loop fusion | flops 8384512 | bytes 16809984 | tf_op jit(solution)/shard_map/while/body/eval_jaxpr/reduce_sum | solution.py:82
  114.3 8.6 %fusion.41 = bf16[8,64,512]{2,1,0:T(8,128)(2,1)} fusion(bf16[1024,8,64]{0,2,1:T(8,128)(2,1)S(1)} %bitcast.278, f32[8,512,1024]{2,1,0:T(8,128)} %get-tuple-element.301, f32[8,512]{1,0:T(8,128)S(1)} %fusion.3, f32[8,512]{1,0:T(8,128)S(1)} %get-tuple-element.300), kind=kOutput, calls=%fused_computation.117 | convolution fusion | flops 549715968 | bytes 18382848 | tf_op jit(solution)/shard_map/while/body/eval_jaxpr/hqk,khd->qhd/dot_general | solution.py:84
  122.9 3.5 fusion.2
  126.4 4.5 fusion.42
  136.8 8.1 %fusion.88 = f32[1024,2048]{1,0:T(8,128)} fusion(bf16[512,2048]{1,0:T(8,128)(2,1)} %all-gather.7.cloned.1.call-done, f32[1024,512]{0,1:T(8,128)} %copy-done.16, f32[512]{0:T(512)S(1)} %bitcast.320, f32[512]{0:T(512)S(1)} %bitcast.308, f32[1024]{0:T(1024)S(1)} %fusion.79, f32[1024]{0:T(1024)S(1)} %broadcast_multiply_fusion.1), kind=kOutput, calls=%fused_computation.221 | convolution fusion | flops 2150105088 | bytes 12595200 | tf_op jit(solution)/shard_map/dot_general | solution.py:41
  144.9 8.6 %fusion.116 = (f32[1024]{0:T(1024)S(1)}, f32[1024,512]{0,1:T(8,128)S(1)}) fusion(f32[512]{0:T(512)S(1)} %bitcast.323, bf16[2048,512]{1,0:T(8,128)(2,1)} %all-gather.9.cloned.1.call-done, f32[1024,2048]{1,0:T(8,128)} %fusion.88, f32[2048]{0:T(1024)S(1)} %bitcast.314, f32[512]{0:T(512)S(1)} %bitcast.321, f32[512]{0:T(512)S(1)} %bitcast.309, ...), kind=kOutput, calls=%fused_computation.242 | convolution fusion | flops 2172124160 | bytes 14706688 | tf_op jit(solution)/shard_map/dot_general | solution.py:41
  160.9 8.8 %fusion.117 = (bf16[2048]{0:T(1024)(128)(2,1)}, bf16[1024,2048]{1,0:T(8,128)(2,1)S(1)}) fusion(f32[1024,2048]{1,0:T(8,128)S(1)} %copy-done.109, f32[2048]{0:T(1024)S(1)} %bitcast.315, bf16[1024,512]{0,1:T(8,128)(2,1)S(1)} %get-tuple-element.253, bf16[2048,512]{1,0:T(8,128)(2,1)S(1)} %copy-done.106), kind=kOutput, calls=%fused_computation.243 | convolution fusion | flops 2193618944 | bytes 15740928 | tf_op jit(solution)/shard_map/dot_general | solution.py:45
  171.7 3.8 convolution_convert_fusion.1
  175.5 7.1 %multiply_reduce_fusion.5 = (bf16[512]{0:T(512)(128)(2,1)}, f32[1024]{0:T(1024)S(1)}, bf16[512]{0:T(512)(128)(2,1)}, f32[1024,512]{0,1:T(8,128)S(1)}) fusion(f32[1024,512]{0,1:T(8,128)S(1)} %copy-done.17, f32[1024]{0:T(1024)S(1)} %fusion.79, f32[1024]{0:T(1024)S(1)} %broadcast_multiply_fusion.1, f32[512]{0:T(512)S(1)} %bitcast.311, ...), kind=kOutput, calls=%fused_computation.62 | convolution fusion | flops 2152724480 | bytes 12603392 | tf_op jit(solution)/shard_map/dot_general | solution.py:45
  188.3 10.3 %multiply_reduce_fusion.3 = (f32[8,512]{1,0:T(8,128)}, f32[8,512,1024]{2,1,0:T(8,128)}) fusion(f32[8,512,1024]{2,1,0:T(8,128)S(1)} %bitcast.231, f32[8,512]{1,0:T(8,128)S(1)} %log_add_fusion.3, bf16[512,8,64]{0,2,1:T(8,128)(2,1)S(1)} %bitcast.262, bf16[1024,8,64]{0,2,1:T(8,128)(2,1)} %bitcast.280), kind=kOutput, calls=%fused_computation.10 | convolution fusion | flops 549449728 | bytes 35160064 | tf_op jit(solution)/shard_map/while/body/eval_jaxpr/qhd,khd->hqk/dot_general | solution.py:104
  198.7 10.5 %multiply_convert_fusion.3 = bf16[8,512,1024]{2,1,0:T(8,128)(2,1)} fusion(f32[8,512,1024]{2,1,0:T(8,128)} %get-tuple-element.312, f32[8,512,1024]{2,1,0:T(8,128)S(1)} %bitcast.231, f32[8,512]{1,0:T(8,128)} %get-tuple-element.311, f32[8,512]{1,0:T(8,128)S(1)} %log_add_fusion.3), kind=kLoop, calls=%fused_computation.9 | loop fusion | flops 16777216 | bytes 41975808 | tf_op jit(solution)/shard_map/while/body/eval_jaxpr/convert_element_type | solution.py:108
  209.2 6.8 %fusion.40 = bf16[512,8,64]{0,2,1:T(8,128)(2,1)} fusion(bf16[1024,8,64]{0,2,1:T(8,128)(2,1)S(1)} %bitcast.248, bf16[8,512,1024]{2,1,0:T(8,128)(2,1)} %multiply_convert_fusion.3), kind=kOutput, calls=%fused_computation.106 | convolution fusion | flops 537395200 | bytes 9961472 | tf_op jit(solution)/shard_map/while/body/eval_jaxpr/hqk,khd->qhd/dot_general | solution.py:110
  216.0 14.7 %multiply_reduce_fusion.2 = (f32[8,512]{1,0:T(8,128)}, f32[8,512,1024]{2,1,0:T(8,128)}) fusion(f32[8,512,1024]{2,1,0:T(8,128)} %get-tuple-element.301, f32[8,512]{1,0:T(8,128)} %log_add_fusion.2, bf16[512,8,64]{0,2,1:T(8,128)(2,1)S(1)} %bitcast.264, bf16[1024,8,64]{0,2,1:T(8,128)(2,1)} %bitcast.281), kind=kOutput, calls=%fused_computation.7 | convolution fusion | flops 549449728 | bytes 35160064 | tf_op jit(solution)/shard_map/while/body/eval_jaxpr/qhd,khd->hqk/dot_general | solution.py:104
  232.8 10.9 %multiply_convert_fusion.2 = bf16[8,512,1024]{2,1,0:T(8,128)(2,1)} fusion(f32[8,512,1024]{2,1,0:T(8,128)} %get-tuple-element.310, f32[8,512,1024]{2,1,0:T(8,128)S(1)} %bitcast.235, f32[8,512]{1,0:T(8,128)} %get-tuple-element.309, f32[8,512]{1,0:T(8,128)} %log_add_fusion.2), kind=kLoop, calls=%fused_computation.6 | loop fusion | flops 16777216 | bytes 41975808 | tf_op jit(solution)/shard_map/while/body/eval_jaxpr/convert_element_type | solution.py:108
  243.8 6.2 %fusion.39 = bf16[512,8,64]{0,2,1:T(8,128)(2,1)S(1)} fusion(bf16[1024,8,64]{0,2,1:T(8,128)(2,1)S(1)} %bitcast.249, bf16[8,512,1024]{2,1,0:T(8,128)(2,1)} %multiply_convert_fusion.2), kind=kOutput, calls=%fused_computation.104 | convolution fusion | flops 537395200 | bytes 9961472 | tf_op jit(solution)/shard_map/while/body/eval_jaxpr/hqk,khd->qhd/dot_general | solution.py:110
  258.7 9.4 %multiply_reduce_fusion.1 = (f32[8,512]{1,0:T(8,128)S(1)}, f32[8,512,1024]{2,1,0:T(8,128)}) fusion(f32[8,512,1024]{2,1,0:T(8,128)S(1)} %bitcast.237, f32[8,512]{1,0:T(8,128)S(1)} %copy-done.71, bf16[512,8,64]{0,2,1:T(8,128)(2,1)S(1)} %bitcast.266, bf16[1024,8,64]{0,2,1:T(8,128)(2,1)} %bitcast.274), kind=kOutput, calls=%fused_computation.4 | convolution fusion | flops 549449728 | bytes 35160064 | tf_op jit(solution)/shard_map/while/body/eval_jaxpr/qhd,khd->hqk/dot_general | solution.py:104
  268.1 10.6 %multiply_convert_fusion.1 = bf16[8,512,1024]{2,1,0:T(8,128)(2,1)} fusion(f32[8,512,1024]{2,1,0:T(8,128)} %get-tuple-element.315, f32[8,512,1024]{2,1,0:T(8,128)S(1)} %bitcast.237, f32[8,512]{1,0:T(8,128)S(1)} %get-tuple-element.314, f32[8,512]{1,0:T(8,128)S(1)} %copy-done.71), kind=kLoop, calls=%fused_computation.3 | loop fusion | flops 16777216 | bytes 41975808 | tf_op jit(solution)/shard_map/while/body/eval_jaxpr/convert_element_type | solution.py:108
  278.7 7.0 %fusion.38 = bf16[512,8,64]{0,2,1:T(8,128)(2,1)} fusion(bf16[1024,8,64]{0,2,1:T(8,128)(2,1)S(1)} %bitcast.244, bf16[8,512,1024]{2,1,0:T(8,128)(2,1)} %multiply_convert_fusion.1), kind=kOutput, calls=%fused_computation.102 | convolution fusion | flops 537395200 | bytes 9961472 | tf_op jit(solution)/shard_map/while/body/eval_jaxpr/hqk,khd->qhd/dot_general | solution.py:110
  288.6 8.9 %fusion.15 = f32[8,64,1024]{2,1,0:T(8,128)} fusion(bf16[512,8,64]{0,2,1:T(8,128)(2,1)S(1)} %bitcast.268, f32[8,512,1024]{2,1,0:T(8,128)} %copy-done.3, f32[8,512]{1,0:T(8,128)S(1)} %copy-done.73), kind=kOutput, calls=%fused_computation.41 | convolution fusion | flops 545259520 | bytes 19415040 | tf_op jit(solution)/shard_map/while/body/eval_jaxpr/hqk,qhd->khd/dot_general | solution.py:120
  297.6 10.0 %multiply_reduce_fusion = (f32[8,512]{1,0:T(8,128)}, f32[8,512,1024]{2,1,0:T(8,128)}) fusion(f32[8,512,1024]{2,1,0:T(8,128)S(1)} %bitcast.241, f32[8,512]{1,0:T(8,128)S(1)} %copy-done.73, bf16[512,8,64]{0,2,1:T(8,128)(2,1)S(1)} %bitcast.269, bf16[1024,8,64]{0,2,1:T(8,128)(2,1)} %bitcast.275), kind=kOutput, calls=%fused_computation.1 | convolution fusion | flops 549449728 | bytes 35160064 | tf_op jit(solution)/shard_map/while/body/eval_jaxpr/qhd,khd->hqk/dot_general | solution.py:104
  307.7 13.7 %multiply_convert_fusion = bf16[8,512,1024]{2,1,0:T(8,128)(2,1)S(1)} fusion(f32[8,512,1024]{2,1,0:T(8,128)} %get-tuple-element.317, f32[8,512,1024]{2,1,0:T(8,128)} %copy-done.3, f32[8,512]{1,0:T(8,128)} %get-tuple-element.316, f32[8,512]{1,0:T(8,128)} %log_add_fusion), kind=kLoop, calls=%fused_computation | loop fusion | flops 16777216 | bytes 41975808 | tf_op jit(solution)/shard_map/while/body/eval_jaxpr/convert_element_type | solution.py:108
  330.6 3.8 bitcast_reduce_fusion.1
  334.4 3.3 fusion.50
  340.5 5.3 fusion.119
  346.0 5.5 convolution_convert_fusion
  351.8 3.5 fusion.54
  355.3 5.3 multiply_convert_fusion.5
  363.2 7.7 %fusion.19 = f32[8,64,1024]{2,1,0:T(8,128)S(1)} fusion(bf16[512,8,64]{0,2,1:T(8,128)(2,1)S(1)} %bitcast.265, f32[8,512,1024]{2,1,0:T(8,128)} %get-tuple-element.301, f32[8,512]{1,0:T(8,128)S(1)} %copy-done.72), kind=kOutput, calls=%fused_computation.43 | convolution fusion | flops 545259520 | bytes 19415040 | tf_op jit(solution)/shard_map/while/body/eval_jaxpr/hqk,qhd->khd/dot_general | solution.py:120
  370.9 3.2 bitcast_reduce_fusion
  376.8 3.2 fusion.60
  387.9 6.0 %reduce-scatter.11.cloned.1.call-done = bf16[256,512]{1,0:T(8,128)(2,1)} async-done(((bf16[2048,512]{1,0:T(8,128)(2,1)}), bf16[256,512]{1,0:T(8,128)(2,1)}) %reduce-scatter.11.cloned.1.call-update) | async-done | bytes 262160 | tf_op jit(solution)/shard_map/reduce_scatter | solution.py:333
  394.0 54.6 %reduce-scatter.7.cloned.1.call-done = bf16[8,64,512]{2,1,0:T(8,128)(2,1)} async-done(((bf16[8,512,512]{2,1,0:T(8,128)(2,1)}), bf16[8,64,512]{2,1,0:T(8,128)(2,1)}) %reduce-scatter.7.cloned.1.call-update) | async-done | bytes 524304 | tf_op jit(solution)/shard_map/reduce_scatter | solution.py:327
  454.1 4.3 convolution_add_fusion
  458.4 3.2 add_add_fusion.3
  461.6 24.1 %reduce-scatter.13.cloned.1.call-done = bf16[64,17]{1,0:T(8,128)(2,1)} async-done(((bf16[512,17]{1,0:T(8,128)(2,1)}), bf16[64,17]{1,0:T(8,128)(2,1)}) %reduce-scatter.13.cloned.1.call-update) | async-done | bytes 2192
  486.6 12.0 %psum.43 = bf16[17,64]{1,0:T(8,128)(2,1)S(1)} all-reduce(bf16[17,64]{1,0:T(8,128)(2,1)S(1)} %copy.117), channel_id=1, replica_groups=mesh['rep'=4,'dp'=8] {'rep'}, use_global_device_ids=true, to_apply=%region_50.51 | all-reduce | flops 1088 | bytes 4352 | tf_op jit(solution)/shard_map/psum | solution.py:324
  499.2 41.8 %all-reduce.3.cloned.1.call-done = (bf16[8,64,512]{2,1,0:T(8,128)(2,1)}, bf16[64,2048]{1,0:T(8,128)(2,1)}, bf16[256,512]{1,0:T(8,128)(2,1)}) async-done(((bf16[8,64,512]{2,1,0:T(8,128)(2,1)}, bf16[64,2048]{1,0:T(8,128)(2,1)}, bf16[256,512]{1,0:T(8,128)(2,1)}), (bf16[8,64,512]{2,1,0:T(8,128)(2,1)}, bf16[64,2048]{1,0:T(8,128)(2,1)}, bf16[256,512]{1,0:T(8,128)(2,1)})) %all-reduce.3.cloned.1.call-update) | async-done | bytes 1048592 | tf_op jit(solution)/shard_map/psum | solution.py:321
  551.8 14.4 %psum.39 = f32[]{:T(128)} all-reduce(f32[]{:T(128)S(6)} %add.374), channel_id=1, replica_groups=mesh['rep'=4,'dp'=8] {'dp'}, use_global_device_ids=true, to_apply=%region_53.54 | all-reduce | flops 1 | bytes 8 | tf_op jit(solution)/shard_map/psum | solution.py:347
  (400 shorter events, 118.6 us)
Async XLA Ops:
  7.2 78.7 %copy-start = (bf16[1024,512]{1,0:T(8,128)(2,1)S(1)}, bf16[1024,512]{1,0:T(8,128)(2,1)}, u32[]{:S(2)}) copy-start(bf16[1024,512]{1,0:T(8,128)(2,1)} %param.21) | copy-start | bytes 3145732
  7.2 19.1 %copy-start.105 = (s32[1,51]{1,0:T(1,128)S(1)}, s32[1,51]{1,0:T(1,128)}, u32[]{:S(2)}) copy-start(s32[1,51]{1,0:T(1,128)} %param.24) | copy-start | bytes 616
  7.2 19.5 %copy-start.67 = (bf16[1024,512]{1,0:T(8,128)(2,1)S(1)}, bf16[1024,512]{1,0:T(8,128)(2,1)}, u32[]{:S(2)}) copy-start(bf16[1024,512]{1,0:T(8,128)(2,1)} %param.19) | copy-start | bytes 3145732
  7.2 21.0 %copy-start.68 = (bf16[1024,512]{1,0:T(8,128)(2,1)S(1)}, bf16[1024,512]{1,0:T(8,128)(2,1)}, u32[]{:S(2)}) copy-start(bf16[1024,512]{1,0:T(8,128)(2,1)} %param.20) | copy-start | bytes 3145732
  7.3 42.8 %all-gather.5.cloned.1.call-start = ((), (), s32[]{:S(2)}) async-start(), calls=%async_computation.4 | async-start | bytes 4718592 | tf_op jit(solution)/shard_map/all_gather | solution.py:207
  9.6 127.2 %all-gather.7.cloned.1.call-start = ((), (), s32[]{:S(2)}) async-start(), calls=%async_computation.5 | async-start | bytes 2359296 | tf_op jit(solution)/shard_map/all_gather | solution.py:208
  11.4 133.4 %all-gather.9.cloned.1.call-start = ((), (), s32[]{:S(2)}) async-start(), calls=%async_computation.6 | async-start | bytes 2359296 | tf_op jit(solution)/shard_map/all_gather | solution.py:209
  13.3 374.7 %reduce-scatter.9.cloned.1.call-start = ((), (), s32[]{:S(2)}) async-start(), calls=%async_computation.8 | async-start | bytes 2359296 | tf_op jit(solution)/shard_map/reduce_scatter | solution.py:330
  25.2 105.6 %copy-start.86 = (f32[1,512]{1,0:T(1,128)}, f32[1,512]{1,0:T(1,128)S(1)}, u32[]{:S(2)}) copy-start(f32[1,512]{1,0:T(1,128)S(1)} %get-tuple-element.286) | copy-start | bytes 6148
  25.3 105.6 %copy-start.99 = (f32[1,512]{1,0:T(1,128)}, f32[1,512]{1,0:T(1,128)S(1)}, u32[]{:S(2)}) copy-start(f32[1,512]{1,0:T(1,128)S(1)} %get-tuple-element.285) | copy-start | bytes 6148
  26.8 131.9 %copy-start.90 = (f32[1,4,4,128]{3,1,2,0:T(4,128)}, f32[1,4,4,128]{3,1,2,0:T(4,128)S(1)}, u32[]{:S(2)}) copy-start(f32[1,4,4,128]{3,1,2,0:T(4,128)S(1)} %copy.118) | copy-start | bytes 24580
  52.4 15.9 %copy-start.34 = (bf16[512,512]{0,1:T(8,128)(2,1)}, bf16[512,512]{0,1:T(8,128)(2,1)S(1)}, u32[]{:S(2)}) copy-start(bf16[512,512]{0,1:T(8,128)(2,1)S(1)} %get-tuple-element.275) | copy-start | bytes 1572868
  54.6 13.7 %copy-start.7 = (bf16[1024,512]{0,1:T(8,128)(2,1)}, bf16[1024,512]{0,1:T(8,128)(2,1)S(1)}, u32[]{:S(2)}) copy-start(bf16[1024,512]{0,1:T(8,128)(2,1)S(1)} %convolution_convert_fusion.5) | copy-start | bytes 3145732
  83.2 47.7 %copy-start.14 = (f32[1024,512]{0,1:T(8,128)}, f32[1024,512]{0,1:T(8,128)S(1)}, u32[]{:S(2)}) copy-start(f32[1024,512]{0,1:T(8,128)S(1)} %get-tuple-element.299) | copy-start | bytes 6291460
  83.5 47.4 %copy-start.81 = (f32[1024]{0:T(1024)}, f32[1024]{0:T(1024)S(1)}, u32[]{:S(2)}) copy-start(f32[1024]{0:T(1024)S(1)} %fusion.78) | copy-start | bytes 12292
  98.8 27.6 %copy-start.1 = (f32[8,512,1024]{2,1,0:T(8,128)}, f32[8,512,1024]{2,1,0:T(8,128)S(1)}, u32[]{:S(2)}) copy-start(f32[8,512,1024]{2,1,0:T(8,128)S(1)} %get-tuple-element.303) | copy-start | bytes 50331652
  114.3 12.1 %copy-start.49 = (bf16[1024,512]{0,1:T(8,128)(2,1)}, bf16[1024,512]{0,1:T(8,128)(2,1)S(1)}, u32[]{:S(2)}) copy-start(bf16[1024,512]{0,1:T(8,128)(2,1)S(1)} %add_convert_fusion.4) | copy-start | bytes 3145732
  175.5 12.8 %slice-start = ((s8[16777216]{0:T(1024)(128)(4,1)}), s8[4194304]{0:T(1024)(128)(4,1)S(1)}, s32[]{:S(2)}) async-start(s8[16777216]{0:T(1024)(128)(4,1)} %bitcast.230), calls=%async_computation.12 | async-start | bytes 8388608
  175.5 12.8 %slice-start.1 = ((s8[16777216]{0:T(1024)(128)(4,1)}), s8[4194304]{0:T(1024)(128)(4,1)S(1)}, s32[]{:S(2)}) async-start(s8[16777216]{0:T(1024)(128)(4,1)} %bitcast.230), calls=%async_computation.13 | async-start | bytes 8388608
  175.5 12.8 %slice-start.2 = ((s8[16777216]{0:T(1024)(128)(4,1)}), s8[4194304]{0:T(1024)(128)(4,1)S(1)}, s32[]{:S(2)}) async-start(s8[16777216]{0:T(1024)(128)(4,1)} %bitcast.230), calls=%async_computation.14 | async-start | bytes 8388608
  188.3 27.8 %copy-start.38 = (bf16[512,512]{0,1:T(8,128)(2,1)}, bf16[512,512]{0,1:T(8,128)(2,1)S(1)}, u32[]{:S(2)}) copy-start(bf16[512,512]{0,1:T(8,128)(2,1)S(1)} %get-tuple-element.272) | copy-start | bytes 1572868
  216.0 14.7 %slice-start.8 = ((s8[16777216]{0:T(1024)(128)(4,1)}), s8[4194304]{0:T(1024)(128)(4,1)S(1)}, s32[]{:S(2)}) async-start(s8[16777216]{0:T(1024)(128)(4,1)} %bitcast.234), calls=%async_computation.20 | async-start | bytes 8388608
  216.0 14.7 %slice-start.9 = ((s8[16777216]{0:T(1024)(128)(4,1)}), s8[4194304]{0:T(1024)(128)(4,1)S(1)}, s32[]{:S(2)}) async-start(s8[16777216]{0:T(1024)(128)(4,1)} %bitcast.234), calls=%async_computation.21 | async-start | bytes 8388608
  216.0 15.6 %slice-start.10 = ((s8[16777216]{0:T(1024)(128)(4,1)}), s8[4194304]{0:T(1024)(128)(4,1)S(1)}, s32[]{:S(2)}) async-start(s8[16777216]{0:T(1024)(128)(4,1)} %bitcast.234), calls=%async_computation.22 | async-start | bytes 8388608
  216.0 16.8 %slice-start.11 = ((s8[16777216]{0:T(1024)(128)(4,1)}), s8[4194304]{0:T(1024)(128)(4,1)S(1)}, s32[]{:S(2)}) async-start(s8[16777216]{0:T(1024)(128)(4,1)} %bitcast.234), calls=%async_computation.23 | async-start | bytes 8388608
  232.8 17.2 %copy-start.15 = (f32[1024,512]{0,1:T(8,128)S(1)}, f32[1024,512]{0,1:T(8,128)}, u32[]{:S(2)}) copy-start(f32[1024,512]{0,1:T(8,128)} %copy-done.14) | copy-start | bytes 6291460
  232.8 17.2 %copy-start.20 = (f32[1024,512]{0,1:T(8,128)S(1)}, f32[1024,512]{0,1:T(8,128)}, u32[]{:S(2)}) copy-start(f32[1024,512]{0,1:T(8,128)} %copy-done.19) | copy-start | bytes 6291460
  243.7 14.9 %slice-start.12 = ((s8[16777216]{0:T(1024)(128)(4,1)}), s8[4194304]{0:T(1024)(128)(4,1)S(1)}, s32[]{:S(2)}) async-start(s8[16777216]{0:T(1024)(128)(4,1)} %bitcast.236), calls=%async_computation.24 | async-start | bytes 8388608
  243.7 14.9 %slice-start.13 = ((s8[16777216]{0:T(1024)(128)(4,1)}), s8[4194304]{0:T(1024)(128)(4,1)S(1)}, s32[]{:S(2)}) async-start(s8[16777216]{0:T(1024)(128)(4,1)} %bitcast.236), calls=%async_computation.25 | async-start | bytes 8388608
  285.7 11.8 %slice-start.20 = ((s8[16777216]{0:T(1024)(128)(4,1)}), s8[4194304]{0:T(1024)(128)(4,1)S(1)}, s32[]{:S(2)}) async-start(s8[16777216]{0:T(1024)(128)(4,1)} %bitcast.240), calls=%async_computation.32 | async-start | bytes 8388608
  285.7 11.8 %slice-start.21 = ((s8[16777216]{0:T(1024)(128)(4,1)}), s8[4194304]{0:T(1024)(128)(4,1)S(1)}, s32[]{:S(2)}) async-start(s8[16777216]{0:T(1024)(128)(4,1)} %bitcast.240), calls=%async_computation.33 | async-start | bytes 8388608
  307.6 86.3 %reduce-scatter.11.cloned.1.call-start = ((), (), s32[]{:S(2)}) async-start(), calls=%async_computation.9 | async-start | bytes 2359296 | tf_op jit(solution)/shard_map/reduce_scatter | solution.py:333
  307.7 13.7 %copy-start.9 = (bf16[1024,512]{0,1:T(8,128)(2,1)S(1)}, bf16[1024,512]{0,1:T(8,128)(2,1)}, u32[]{:S(2)}) copy-start(bf16[1024,512]{0,1:T(8,128)(2,1)} %copy-done.7) | copy-start | bytes 3145732
  307.7 16.4 %copy-start.12 = (f32[8,64,1024]{2,1,0:T(8,128)S(1)}, f32[8,64,1024]{2,1,0:T(8,128)}, u32[]{:S(2)}) copy-start(f32[8,64,1024]{2,1,0:T(8,128)} %fusion.118) | copy-start | bytes 6291460
  351.5 97.0 %reduce-scatter.7.cloned.1.call-start = ((), (), s32[]{:S(2)}) async-start(), calls=%async_computation.7 | async-start | bytes 4718592 | tf_op jit(solution)/shard_map/reduce_scatter | solution.py:327
  355.3 15.6 %slice-start.4 = ((s8[16777216]{0:T(1024)(128)(4,1)}), s8[4194304]{0:T(1024)(128)(4,1)S(1)}, s32[]{:S(2)}) async-start(s8[16777216]{0:T(1024)(128)(4,1)} %bitcast.232), calls=%async_computation.16 | async-start | bytes 8388608
  355.3 15.6 %slice-start.5 = ((s8[16777216]{0:T(1024)(128)(4,1)}), s8[4194304]{0:T(1024)(128)(4,1)S(1)}, s32[]{:S(2)}) async-start(s8[16777216]{0:T(1024)(128)(4,1)} %bitcast.232), calls=%async_computation.17 | async-start | bytes 8388608
  380.0 105.8 %reduce-scatter.13.cloned.1.call-start = ((), (), s32[]{:S(2)}) async-start(), calls=%async_computation.10 | async-start | bytes 147456
  381.6 159.4 %all-reduce.3.cloned.1.call-start = ((), (), s32[]{:S(2)}) async-start(), calls=%async_computation.11 | async-start | bytes 2097152 | tf_op jit(solution)/shard_map/psum | solution.py:321
  384.8 63.8 %copy-start.41 = (bf16[512,8,64]{0,2,1:T(8,128)(2,1)S(1)}, bf16[512,8,64]{0,2,1:T(8,128)(2,1)}, u32[]{:S(2)}) copy-start(bf16[512,8,64]{0,2,1:T(8,128)(2,1)} %fusion.38) | copy-start | bytes 1572868
  384.8 63.8 %copy-start.43 = (bf16[512,8,64]{0,2,1:T(8,128)(2,1)S(1)}, bf16[512,8,64]{0,2,1:T(8,128)(2,1)}, u32[]{:S(2)}) copy-start(bf16[512,8,64]{0,2,1:T(8,128)(2,1)} %copy-done.42) | copy-start | bytes 1572868
  461.6 105.3 %copy-start.76 = (f32[17,64]{1,0:T(8,128)S(1)}, f32[17,64]{1,0:T(8,128)}, u32[]{:S(2)}) copy-start(f32[17,64]{1,0:T(8,128)} %param.35) | copy-start | bytes 13060
  461.6 105.3 %copy-start.83 = (f32[17,64]{1,0:T(8,128)S(1)}, f32[17,64]{1,0:T(8,128)}, u32[]{:S(2)}) copy-start(f32[17,64]{1,0:T(8,128)} %param.37) | copy-start | bytes 13060
  461.6 105.4 %copy-start.84 = (f32[17,64]{1,0:T(8,128)S(1)}, f32[17,64]{1,0:T(8,128)}, u32[]{:S(2)}) copy-start(f32[17,64]{1,0:T(8,128)} %param.36) | copy-start | bytes 13060
  461.6 106.0 %copy-start.56 = (f32[256,512]{1,0:T(8,128)S(1)}, f32[256,512]{1,0:T(8,128)}, u32[]{:S(2)}) copy-start(f32[256,512]{1,0:T(8,128)} %param.32) | copy-start | bytes 1572868
  546.2 24.3 %copy-start.57 = (f32[64,2048]{1,0:T(8,128)S(1)}, f32[64,2048]{1,0:T(8,128)}, u32[]{:S(2)}) copy-start(f32[64,2048]{1,0:T(8,128)} %param.29) | copy-start | bytes 1572868
  546.2 24.3 %copy-start.66 = (bf16[64,2048]{1,0:T(8,128)(2,1)S(1)}, bf16[64,2048]{1,0:T(8,128)(2,1)}, u32[]{:S(2)}) copy-start(bf16[64,2048]{1,0:T(8,128)(2,1)} %get-tuple-element.234) | copy-start | bytes 786436
  551.8 21.4 %copy-start.50 = (f32[8,64,512]{2,1,0:T(8,128)S(1)}, f32[8,64,512]{2,1,0:T(8,128)}, u32[]{:S(2)}) copy-start(f32[8,64,512]{2,1,0:T(8,128)} %param.26) | copy-start | bytes 3145732
  (97 other events, 516.1 us)
Sparse Core Ops, SparseCore 0:
  10.6 39.4 all-gather.4
  52.5 27.9 all-gather.6
  82.9 27.9 all-gather.8
  307.8 41.4 reduce-scatter.8
  352.7 41.1 reduce-scatter.10
  397.2 51.3 reduce-scatter.6
  452.4 33.3 reduce-scatter.12
  488.3 52.5 all-reduce.2
where the time goes:
time: 588 us; the launch traced here: 584 us
  matrix products  246 us (42%)
  waiting for transfers between devices  141 us (24%)
  other arithmetic  108 us (18%)
  blocking collectives  37 us (6%)
  local copies, waits for them, and re-layouts  30.9 us (5%)
  between operations  20.5 us (3%)
    reduce_scatter x1, waiting for transfers between devices, per_device(): lax.psum_scatter(summed[0].astype(jnp.bfloat16), 'dp', scatter_dimension=...  54.6 us
    convert_element_type x4, other arithmetic, attend_back(): score_grad = (shares * (share_grad - inner)).astype(jnp.bfloat16)  45.8 us
    dot_general x4, matrix products, attend_back(): jnp.einsum('qhd,khd->hqk', grad_block, value_rows, preferred_element_type...  44.5 us
    psum x1, waiting for transfers between devices, per_device(): lax.psum(attention_raw.astype(jnp.bfloat16), 'rep').astype(jnp.float32)  41.8 us
    dot_general x10, matrix products, back_project(): lax.dot_general(grads, matrix, (((1,), (1,)), ((), ())), preferred_elemen...  39.4 us
    dot_general x10, matrix products, project(): return jnp.dot(inputs, matrix, preferred_element_type=jnp.float32)  33.9 us
    unnamed x283, local copies, waits for them, and re-layouts  29.4 us
    dot_general x10, matrix products, outer_sum(): lax.dot_general(left, right, (((0,), (0,)), ((), ())), preferred_element_...  28.4 us
  transfers between devices with their start and end apart: 8, of which 5 were waited for; matrix products, arithmetic and copies ran while one was open for 34% of the time, Pallas kernels for 0%

commit v1 on v0

v1 whole, which is shorter than its diff:
```python
import functools
import math

import jax
import jax.numpy as jnp
from jax import lax
from jax.experimental import pallas as pl
from jax.experimental.pallas import tpu as pltpu
from jax.sharding import PartitionSpec as P

H = 8
STEP = 10
NORM_EPS = 1e-05
CLIP_NORM = 1.0
BETA_ONE = 0.9
BETA_TWO = 0.999
ADAM_EPS = 1e-08
WEIGHT_DECAY = 0.01
RATE_MATRIX = 0.03
RATE_VECTOR = 0.5
NEG_FILL = -1000000000.0
GELU_C = math.sqrt(2.0 / math.pi)
GELU_A = 0.044715
LOG2_E = math.log2(math.e)
NEG_TWO = NEG_FILL * LOG2_E
F32 = jnp.float32
LOW = jnp.bfloat16
MIB = 1 << 20
MESH = pl.DeviceIdType.MESH


def nn(left, right):
    return jnp.dot(left, right, preferred_element_type=F32)


def nt(left, right):
    return lax.dot_general(left, right, (((1,), (1,)), ((), ())), preferred_element_type=F32)


def tn(left, right):
    return lax.dot_general(left, right, (((0,), (0,)), ((), ())), preferred_element_type=F32)


def fold(values, op):
    rows = min(values.shape[0], 64 if values.shape[1] <= 256 else 32)
    total = values[0:rows]
    for i in range(1, values.shape[0] // rows):
        total = op(total, values[i * rows : (i + 1) * rows])
    while rows > 8:
        rows //= 2
        total = op(total[0:rows], total[rows : 2 * rows])
    return total


def colmax(values):
    return jnp.max(fold(values, jnp.maximum), axis=0, keepdims=True)


def colsum(values):
    return jnp.sum(fold(values.astype(F32), jnp.add), axis=0, keepdims=True)


def wide(column, width):
    return jnp.concatenate([column] * (width // 128), axis=1)


def normed(values):
    centred = values - jnp.mean(values, axis=-1, keepdims=True)
    rs = lax.rsqrt(jnp.mean(centred * centred, axis=-1, keepdims=True) + NORM_EPS)
    return centred * rs, rs


def norm_back(grad, xh, rs):
    first = jnp.mean(grad, axis=-1, keepdims=True)
    second = jnp.mean(grad * xh, axis=-1, keepdims=True)
    return rs * (grad - first - xh * second)


def step_kernel(
    nd, nr,
    seg, ham, pri, vec_w, dec, tgt, enc, cot, aw_h, ew_h, cw_h,
    out_h, ig_h, eg_h, ga_h, ge_h, gc_h, gvec, norm,
    wself, watt, w1, w2, x, e, qs, ks, vs, os, qc, kcr, vc, oc, xh1, rs1, h1, h2, z, du, df, dr, da, tb, tt,
    gcol, scol, lt, lterms, dterms, vec, vacc, gp, acc_k, acc_v, hamp,
    g1, g2, gcr, gse, gvo, gwo, gve, r1p, r2p, rzp, r1o, r2o, rzo, r1v, r2v, rzv, rze, rzc, zs, zv,
    vslots, nall,
    sems, gather_sems, reduce_sems, direct_sems, norm_sems, ready,
):
    tokens, width = x.shape
    hidden = du.shape[1]
    pairs = width // 128
    bt = 256
    blocks = tokens // bt
    wide_bt = min(512, tokens)
    wide_blocks = tokens // wide_bt
    slots = ham.shape[1]
    spots = nd // 2
    r = width // nd
    me = lax.axis_index("dp")
    rep = lax.axis_index("rep")
    spot, core = me // 2, me % 2

    def core_peer():
        return {"dp": me + 1 - 2 * core}

    def spot_at(o):
        return (spot + o) % spots

    def plane_peer(o):
        return {"dp": 2 * spot_at(o) + core}

    half = nr // 2
    low_side = rep < half
    to_centre = jnp.where(low_side, half - 1 - rep, rep - half)
    is_centre = to_centre == 0
    is_end = to_centre == half - 1
    not_centre = to_centre > 0
    not_end = to_centre < half - 1
    inward = {"rep": jnp.where(low_side, rep + 1, rep - 1)}
    outward = {"rep": jnp.where(low_side, rep - 1, rep + 1)}
    dp_peers = [{"dp": (me + o) % nd} for o in range(1, nd)]

    rep_peers = [{"rep": (rep + o) % nr} for o in range(1, nr)]

    def signal_all(sem):
        for peer in dp_peers + rep_peers:
            pl.semaphore_signal(sem, inc=1, device_id=peer, device_id_type=MESH)

    def wait_all(sem):
        pl.semaphore_wait(sem, len(dp_peers + rep_peers))

    def remote(src, dst, send, recv, peer):
        return pltpu.make_async_remote_copy(
            src_ref=src, dst_ref=dst, send_sem=send, recv_sem=recv, device_id=peer, device_id_type=MESH
        )

    def wait_bytes(ref, sem):
        pltpu.make_async_copy(ref, ref, sem).wait()

    def copy(i, src, dst):
        return pltpu.make_async_copy(src, dst, sems.at[i])

    proj_s, proj_c = (qs, ks, vs, os), (qc, kcr, vc, oc)
    third = 3 * 128
    load_att = copy(4, aw_h, xh1.at[pl.ds(0, 8 * r), :])
    chunks = hidden // width
    load_exp = [
        copy(8 + j, ew_h.at[:, pl.ds(j * width, width)], xh1.at[pl.ds((12 + j) * r, r), :])
        for j in range(chunks)
    ]
    load_con = copy(6, cw_h, xh1.at[pl.ds(8 * r, 4 * r), :])
    loads = [copy(0, dec, x), copy(1, tgt, tb), copy(2, enc, e), copy(3, cot, dr)]
    for c in [load_att] + loads[:2] + load_exp + [load_con] + loads[2:]:
        c.start()

    barrier = pltpu.get_barrier_semaphore()
    signal_all(barrier)

    def rows_of(i, size=bt):
        return pl.ds(pl.multiple_of(i * size, size), size)

    def loop(count, body):
        def wrapped(i, carry):
            body(i)
            return carry
        lax.fori_loop(0, count, wrapped, 0)

    def third_of(p):
        return pl.ds(pl.multiple_of(p * third, 128), third)

    def side(buf_width, k):
        part = buf_width // 2
        return pl.ds(pl.multiple_of(k * part, 128), part)

    groups = [
        (lambda q, b, p: vslots.at[q, b]),
        (lambda q, b, p: watt.at[pl.ds(0, 2), q, b]),
        (lambda q, b, p: watt.at[pl.ds(2, 3), q, b]),
        (lambda q, b, p: w1.at[q, b]),
        (lambda q, b, p: w2.at[q, b]),
        (lambda q, b, p: wself.at[q, b, :, third_of(p)]),
    ]
    halves = [
        None,
        (lambda q, b, k: watt.at[pl.ds(0, 2), q, b, :, side(width, k)]),
        (lambda q, b, k: watt.at[pl.ds(2, 3), q, b, :, side(width, k)]),
        (lambda q, b, k: w1.at[q, b, :, side(hidden, k)]),
        (lambda q, b, k: w2.at[q, b, :, side(width, k)]),
    ]
    my_half = rep % 2
    twin = {"rep": rep + 1 - 2 * (rep % 2)}
    qkv = 5
    every = pl.ds(0, spots)
    others = pl.ds(0, spots - 1)

    def plane_part(i, q, b, p):
        return groups[i](q, b, p) if i in (0, qkv) else halves[i](q, b, my_half)

    def send_group(i, p=0):
        own = plane_part(i, spot, core, p)
        for o in range(1, spots):
            remote(own, own, gather_sems.at[0, i + p], gather_sems.at[1, i + p], plane_peer(o)).start()

    def pass_group(i):
        wait_bytes(halves[i](others, 0, 0), gather_sems.at[1, i])
        for o in range(1, spots):
            got = halves[i](spot_at(o), core, my_half)
            remote(got, got, gather_sems.at[4, i], gather_sems.at[5, i], twin).start()

    def forward_group(i, p=0):
        if i in (0, qkv):
            wait_bytes(groups[i](others, 0, p), gather_sems.at[1, i + p])
        else:
            wait_bytes(halves[i](others, 0, 0), gather_sems.at[5, i])
        mine = groups[i](every, core, p)
        remote(mine, mine, gather_sems.at[2, i + p], gather_sems.at[3, i + p], core_peer()).start()

    def use_group(i, p=0):
        wait_bytes(groups[i](every, 0, p), gather_sems.at[3, i + p])

    def finish_group(i, p=0):
        wait_bytes(groups[i](every, 0, p), gather_sems.at[2, i + p])
        if i in (0, qkv):
            wait_bytes(groups[i](others, 0, p), gather_sems.at[0, i + p])
        else:
            wait_bytes(halves[i](others, 0, 0), gather_sems.at[0, i])
            wait_bytes(halves[i](others, 0, 0), gather_sems.at[4, i])

    own_width = vec_w.shape[1]
    vslots[spot, core] = jnp.zeros(vslots.shape[2:], LOW)
    vec[...] = jnp.zeros_like(vec)
    vec[0 : vec_w.shape[0], 0:own_width] = vec_w[...]
    vslots[spot, core] = vec[:, 0:128].astype(LOW)

    def cast_att(first, count):
        for k in range(first, first + count):
            watt[k - 3, spot, core] = xh1[k * r : (k + 1) * r, :].astype(LOW)

    load_att.wait()
    for p in range(pairs):
        for k in range(3):
            at = p * third + k * 128
            wself[spot, core, :, at : at + 128] = xh1[
                k * r : (k + 1) * r, p * 128 : (p + 1) * 128
            ].astype(LOW)
    wait_all(barrier)
    send_group(0)
    for p in range(pairs):
        send_group(qkv, p)
    cast_att(3, 2)
    send_group(1)
    cast_att(5, 3)
    send_group(2)
    for j in range(chunks):
        load_exp[j].wait()
        w1[spot, core, :, j * width : (j + 1) * width] = xh1[
            (12 + j) * r : (13 + j) * r, :
        ].astype(LOW)
    send_group(3)
    load_con.wait()
    w2[spot, core] = xh1[8 * r : 12 * r, :].astype(LOW)
    send_group(4)

    vacc[...] = jnp.zeros_like(vacc)
    seg_row = seg[...].astype(F32)
    slot_pad = (slots + 63) // 64 * 64
    slot_ids = lax.broadcasted_iota(jnp.int32, (slot_pad, tokens), 0).astype(F32)
    member = jnp.where(slot_ids == seg_row, 1.0, 0.0)
    length = jnp.sum(member * jnp.sum(member, axis=1, keepdims=True), axis=0, keepdims=True)
    hamp[...] = jnp.zeros_like(hamp)
    hamp[0:1, 0:slots] = ham[...].astype(F32)
    distance = nn(hamp[:, 0:slot_pad].astype(LOW), member.astype(LOW))[0:1]
    glanced = jnp.where(
        2.0 * pri[...].astype(F32) * length < distance * float(tokens), 1.0, 0.0
    )
    gcol[...] = jnp.broadcast_to(glanced, (128, tokens)).T
    scol[...] = jnp.broadcast_to(seg_row, (128, tokens)).T

    lane = lax.broadcasted_iota(jnp.int32, (1, 128), 1)
    mask_f = (jnp.where(lane < 64, 1.0, 0.0), jnp.where(lane < 64, 0.0, 1.0))
    mask = (mask_f[0].astype(LOW), mask_f[1].astype(LOW))
    is_low = lane < 64

    def lanes_of(p):
        return pl.ds(pl.multiple_of(p * 128, 128), 128)

    for c in loads[:2]:
        c.wait()

    def choose(i):
        rows = rows_of(i)
        x[rows, :] = jnp.where(
            wide(gcol[rows, :], width) > 0.5, tb[rows, :].astype(F32), x[rows, :].astype(F32)
        ).astype(LOW)

    loop(blocks, choose)

    forward_group(0)
    forward_group(qkv, 0)
    use_group(0)
    vec_sum = jnp.zeros(vec.shape, F32)
    src_lane = lax.broadcasted_iota(jnp.int32, (128, width), 0)
    dst_lane = lax.broadcasted_iota(jnp.int32, (128, width), 1)
    for d in range(nd):
        pick = jnp.where(
            (dst_lane == src_lane + d * own_width) & (src_lane < own_width), 1.0, 0.0
        ).astype(LOW)
        vec_sum = vec_sum + nn(vslots[d // 2, d % 2], pick)
    vec[...] = vec_sum

    def att_w(k):
        return watt[k - 3].reshape(width, width)

    def exp_w(j):
        return w1[:, :, :, j * width : (j + 1) * width].reshape(width, width)

    per = spots * width // hidden

    def con_w(j):
        return w2[j * per : (j + 1) * per].reshape(width, width)

    def self_in(p):
        lanes = lanes_of(p)
        pair_w = wself[:, :, :, third_of(p)].reshape(width, third)
        bias_q, bias_v = vec[6:7, lanes], vec[7:8, lanes]

        def block(i):
            rows = rows_of(i, wide_bt)
            made = nn(x[rows, :], pair_w)
            proj_s[0][rows, lanes] = ((made[:, 0:128] + bias_q) * (0.125 * LOG2_E)).astype(LOW)
            proj_s[1][rows, lanes] = made[:, 128:256].astype(LOW)
            proj_s[2][rows, lanes] = (made[:, 256:384] + bias_v).astype(LOW)

        loop(wide_blocks, block)

    qb = 256

    term_id = lane % 4

    def term_lanes(p):
        return ((lane % 64) // 4 == p) & (term_id < 3)

    def minus_terms(values):
        first = values.astype(LOW).astype(F32)
        second = (values - first).astype(LOW).astype(F32)
        third_term = values - first - second
        return -jnp.where(term_id == 0, first, jnp.where(term_id == 1, second, third_term))

    lterms[...] = jnp.zeros_like(lterms)
    ones_rows = jnp.ones((16, tokens), LOW)
    upper_rows = lax.broadcasted_iota(jnp.int32, (128, qb), 0) >= 64

    def attend(proj, which, before, after):
        def pair(p):
            before(p)
            lanes = lanes_of(p)
            keys = proj[1][:, lanes]
            turned = proj[2][:, lanes].T
            sides = [jnp.concatenate([turned[k : k + 64], ones_rows], axis=0) for k in (0, 64)]
            units = [(b, head) for b in range(tokens // qb) for head in (0, 1)]

            def scores_of(unit):
                b, head = unit
                return nt(keys, proj[0][b * qb : (b + 1) * qb, lanes] * mask[head])

            ahead = scores_of(units[0])
            for k, (b, head) in enumerate(units):
                scores = ahead
                if k + 1 < len(units):
                    ahead = scores_of(units[k + 1])
                rows = pl.ds(b * qb, qb)
                if head == 0:
                    logs, mixes = [], []
                same = wide(scol[...], qb) == seg_row[:, b * qb : (b + 1) * qb]
                scores = jnp.where(same, scores, NEG_TWO)
                top = colmax(scores)
                mixed = nn(sides[head], jnp.exp2(scores - top).astype(LOW))
                total = mixed[64:65]
                mixes.append(mixed[0:64] * (1.0 / total))
                logs.append(top + jnp.log2(total))
                lt[which, 2 * p + head, :, rows] = NEG_TWO - logs[head]
                if head == 0:
                    continue
                proj[3][rows, lanes] = jnp.concatenate(mixes, axis=0).T.astype(LOW)
                spread = jnp.where(upper_rows, logs[0], logs[1]).T
                lterms[which, rows, :] = jnp.where(
                    term_lanes(p), minus_terms(spread), lterms[which, rows, :].astype(F32)
                ).astype(LOW)
            after(p)
        loop(pairs, pair)

    def self_before(p):
        use_group(qkv, p)
        self_in(p)

        @pl.when(p < pairs - 1)
        def _():
            forward_group(qkv, p + 1)

    def self_hook(p):
        @pl.when(p == 0)
        def _():
            pass_group(1)

        @pl.when(p == 1)
        def _():
            pass_group(2)

        @pl.when(p == pairs - 2)
        def _():
            forward_group(1)
            pass_group(3)

        @pl.when(p == pairs - 1)
        def _():
            forward_group(2)

    attend(proj_s, 0, self_before, self_hook)
    use_group(1)
    use_group(2)
    loads[2].wait()

    def first_norm(i):
        rows = rows_of(i)
        total = x[rows, :].astype(F32) + nn(proj_s[3][rows, :], att_w(3)) + vec[8:9, :]
        xh, rs = normed(total)
        xh1[rows, :] = xh
        rs1[rows, :] = rs
        low = (xh * vec[0:1, :] + vec[1:2, :]).astype(LOW)
        h1[rows, :] = low
        proj_c[0][rows, :] = ((nn(low, att_w(4)) + vec[9:10, :]) * (0.125 * LOG2_E)).astype(LOW)

        enc_low = e[rows, :]
        proj_c[1][rows, :] = nn(enc_low, att_w(5)).astype(LOW)
        proj_c[2][rows, :] = (nn(enc_low, att_w(6)) + vec[10:11, :]).astype(LOW)

    loop(blocks, first_norm)
    pass_group(4)

    def cross_hook(p):
        @pl.when(p == 1)
        def _():
            forward_group(3)

        @pl.when(p == pairs - 2)
        def _():
            forward_group(4)

    attend(proj_c, 1, lambda p: None, cross_hook)

    loads[3].wait()
    use_group(3)
    use_group(4)
    def add_row(k, value):
        vacc[k : k + 1, :] += value

    def feed_forward(i):
        rows = rows_of(i)
        valid = jnp.where(wide(scol[rows, :], width) >= 0.0, 1.0, 0.0)
        start = xh1[rows, :] * vec[0:1, :] + vec[1:2, :]
        xh2, rs2 = normed(start + nn(proj_c[3][rows, :], att_w(7)) + vec[11:12, :])
        second = xh2 * vec[2:3, :] + vec[3:4, :]
        low = second.astype(LOW)
        tt[:, rows] = low.T
        branch_sum = second + vec[12:13, :]
        for j in range(chunks):
            cols = pl.ds(j * width, width)
            u = nn(low, exp_w(j)) + vec[13 + j : 14 + j, :]
            square = u * u
            th = jnp.tanh(GELU_C * u * (1.0 + GELU_A * square))
            half = 0.5 * (1.0 + th)
            z[rows, cols] = (u * half).astype(LOW)
            gp[:, cols] = (
                half + u * half * (1.0 - th) * (GELU_C * (1.0 + 3.0 * GELU_A * square))
            ).astype(LOW)
        xh3, rs3 = normed(branch_sum + nn(z[rows, :], w2[...].reshape(hidden, width)))
        tb[rows, :] = (xh3 * vec[4:5, :] + vec[5:6, :]).astype(LOW)
        grad = dr[rows, :] * valid
        add_row(5, colsum(grad))
        add_row(4, colsum(grad * xh3))
        third = norm_back(grad * vec[4:5, :], xh3, rs3)
        branch = third.astype(LOW)
        df[rows, :] = branch
        add_row(12, colsum(branch))
        for j in range(chunks):
            cols = pl.ds(j * width, width)
            inner = (nt(branch, con_w(j)) * gp[:, cols]).astype(LOW)
            du[rows, cols] = inner
            add_row(13 + j, colsum(inner))
        grad = third + nt(du[rows, :], w1[...].reshape(width, hidden))
        add_row(3, colsum(grad))
        add_row(2, colsum(grad * xh2))
        grad = norm_back(grad * vec[2:3, :], xh2, rs2)
        dr[rows, :] = grad
        low = grad.astype(LOW)
        da[rows, :] = low
        add_row(11, colsum(low))

    loop(blocks, feed_forward)
    out_copy = copy(0, tb, out_h)
    out_copy.start()
    for i in range(qkv):
        finish_group(i)
    for p in range(pairs):
        finish_group(qkv, p)
    signal_all(ready)

    def first_step(g):
        buf, one, _, _, sid = g
        remote(buf.at[:, 1 - core], one, reduce_sems.at[0, sid], reduce_sems.at[1, sid], core_peer()).start()

    def second_step(g):
        buf, one, two, _, sid = g
        wait_bytes(one, reduce_sems.at[1, sid])
        for q in range(spots):
            buf[q, core] = (buf[q, core].astype(F32) + one[q].astype(F32)).astype(LOW)
        for o in range(1, spots):
            remote(
                buf.at[spot_at(o), core], two.at[o - 1],
                reduce_sems.at[2, sid], reduce_sems.at[3, sid], plane_peer(o),
            ).start()

    def third_step(g):
        buf, _, two, (up, _), sid = g
        wait_bytes(two, reduce_sems.at[3, sid])
        total = buf[spot, core].astype(F32)
        for o in range(spots - 1):
            total = total + two[o].astype(F32)
        buf[spot, core] = total.astype(LOW)

        @pl.when(is_end & not_centre)
        def _():
            remote(buf.at[spot, core], up, reduce_sems.at[4, sid], reduce_sems.at[5, sid], inward).start()

    def fourth_step(g):
        buf, _, _, (up, down), sid = g
        own = buf.at[spot, core]

        @pl.when(not_end)
        def _():
            wait_bytes(up, reduce_sems.at[5, sid])
            buf[spot, core] = (own[...].astype(F32) + up[...].astype(F32)).astype(LOW)

        @pl.when(not_end & not_centre)
        def _():
            remote(own, up, reduce_sems.at[4, sid], reduce_sems.at[5, sid], inward).start()

        @pl.when(is_centre)
        def _():
            remote(own, down, reduce_sems.at[6, sid], reduce_sems.at[7, sid], inward).start()

    def fifth_step(g):
        buf, _, _, (up, down), sid = g

        @pl.when(is_centre)
        def _():
            wait_bytes(down, reduce_sems.at[7, sid])
            down[...] = (buf[spot, core].astype(F32) + down[...].astype(F32)).astype(LOW)

        @pl.when(is_centre & not_end)
        def _():
            remote(down, down, reduce_sems.at[8, sid], reduce_sems.at[9, sid], outward).start()

    def final_step(g):
        _, _, _, (up, down), sid = g

        @pl.when(not_centre)
        def _():
            wait_bytes(down, reduce_sems.at[9, sid])

        @pl.when(not_centre & not_end)
        def _():
            remote(down, down, reduce_sems.at[8, sid], reduce_sems.at[9, sid], outward).start()

        return down[...]

    def finish_sends(g):
        _, one, two, (up, down), sid = g
        wait_bytes(one, reduce_sems.at[0, sid])
        wait_bytes(two, reduce_sems.at[2, sid])

        @pl.when(not_centre)
        def _():
            wait_bytes(up, reduce_sems.at[4, sid])

        @pl.when(is_centre)
        def _():
            wait_bytes(down, reduce_sems.at[6, sid])

        @pl.when(not_end)
        def _():
            wait_bytes(down, reduce_sems.at[8, sid])

    def third_direct(g, every_rep, k):
        buf, _, two, _, sid = g
        wait_bytes(two, reduce_sems.at[3, sid])
        total = buf[spot, core].astype(F32)
        for o in range(spots - 1):
            total = total + two[o].astype(F32)
        every_rep[rep] = total.astype(LOW)
        for peer in rep_peers:
            own = every_rep.at[rep]
            remote(own, own, direct_sems.at[0, k], direct_sems.at[1, k], peer).start()

    def final_direct(every_rep, k):
        wait_bytes(every_rep.at[pl.ds(0, nr - 1)], direct_sems.at[1, k])
        total = every_rep[0].astype(F32)
        for q in range(1, nr):
            total = total + every_rep[q].astype(F32)
        return total

    def finish_direct(g, every_rep, k):
        _, one, two, _, sid = g
        wait_bytes(one, reduce_sems.at[0, sid])
        wait_bytes(two, reduce_sems.at[2, sid])
        wait_bytes(every_rep.at[pl.ds(0, nr - 1)], direct_sems.at[0, k])

    steps = (first_step, second_step, third_step, fourth_step, fifth_step)
    chunks_of = [pl.ds(j * width, width) for j in range(chunks)]
    rows_in = [pl.ds(j * r, r) for j in range(chunks)]
    grps = {}
    for j in range(chunks):
        c = chunks_of[j]
        grps["e", j] = (
            g1.at[:, :, :, c], w1.at[:, 0, :, c], w1.at[others, 1, :, c],
            (w1.at[spots - 1, 1, :, c], rze.at[:, c]), j,
        )
        c = rows_in[j]
        grps["c", j] = (
            g2.at[:, :, c], w2.at[:, 0, c], w2.at[others, 1, c],
            (w2.at[spots - 1, 1, c], rzc.at[c]), chunks + j,
        )
    for k, (name, buf) in enumerate((("vo", gvo), ("wo", gwo))):
        grps[name, 0] = (buf, r1o.at[k], r2o.at[k], (rzo.at[k, 0], rzo.at[k, 1]), 2 * chunks + k)
    grps["v", 0] = (gve, r1v, r2v, (rzv.at[0], rzv.at[1]), 2 * chunks + 2)
    for i in range(2 * pairs):
        name, buf = ("x", gcr) if i < pairs else ("s", gse)
        grps[name, i % pairs] = (
            buf.at[i % pairs], r1p.at[i], r2p.at[i], (rzp.at[i, 0], rzp.at[i, 1]), 2 * chunks + 3 + i,
        )

    def run_steps(text):
        for word in text:
            step, name = int(word[0]), word[1:]
            ids = range(chunks) if name in ("e", "c") else [0]
            if name[-1].isdigit():
                name, ids = name[:-1], [int(name[-1])]
            for k in ids:
                if (name, k) in grps:
                    steps[step - 1](grps[name, k])

    def run_table(table, p):
        for k, text in enumerate(table):
            if text:
                pl.when(p == k)(functools.partial(run_steps, text))

    def contract_grads(j):
        cols = pl.ds(pl.multiple_of(j * width, width), width)
        g2[pl.ds(j * per, per)] = tn(z[:, cols], df[...]).astype(LOW).reshape(per, 2, 4 * r, width)

    loop(chunks, contract_grads)
    wait_all(ready)
    run_steps(("1c",))

    def expand_grads(j):
        cols = pl.ds(pl.multiple_of(j * width, width), width)
        g1[:, :, :, cols] = nn(tt[...], du[:, cols]).astype(LOW).reshape(spots, 2, r, width)
        run_table([("1e0",), ("1e1", "2c0",), ("1e2", "2c1",), ("1e3", "2c2",)], j)

    loop(chunks, expand_grads)
    gvo[...] = tn(proj_c[3][...], da[...]).astype(LOW).reshape(spots, 2, r, width)
    run_steps(("1vo", "2c3", "2e0",))

    def part(buf, i):
        return buf.at[:, pl.ds(i * width, width)]

    do = part(z, 3)
    kt = du.at[pl.ds(0, width), pl.ds(0, tokens)]
    xt = du.at[pl.ds(0, width), pl.ds(tokens, tokens)]
    et = du.at[pl.ds(tokens // 2, width), pl.ds(0, tokens)]

    head_of = lax.broadcasted_iota(jnp.int32, (width, 128), 0) // 64
    place = lax.broadcasted_iota(jnp.int32, (width, 128), 1)
    sel = jnp.where(
        (head_of == (place % 64) // 4 * 2 + 1 - place // 64) & (place % 4 < 3), 1.0, 0.0
    ).astype(LOW)

    def before_attention(proj, base, rows, grad_low):
        mixed = nt(grad_low, att_w(base + 3)).astype(LOW)
        do[rows, :] = mixed
        prod = mixed.astype(F32) * proj[3][rows, :].astype(F32)
        high = prod.astype(LOW)
        rest = (prod - high.astype(F32)).astype(LOW)
        dterms[rows, :] = minus_terms(nn(high, sel) + nn(rest, sel)).astype(LOW)
        kt[:, rows] = proj[1][rows, :].T

    kb = kc = 256

    def attend_back(proj, which, places, hook, after):
        def pair(p):
            lanes = lanes_of(p)
            dq, dk, dv = places(p)
            acc_k[...] = jnp.zeros_like(acc_k)
            acc_v[...] = jnp.zeros_like(acc_v)
            ones = jnp.where(term_lanes(p), 1.0, 0.0).astype(LOW)
            ones_at = [ones * mask[1], ones * mask[0]]

            def stretch(i):
                units = [(b, c) for b in range(2) for c in range(tokens // kc)]
                made = {}

                def operands(b):
                    rows = rows_of(2 * i + b, kb)
                    queries = proj[0][rows, lanes]
                    grads = do[rows, lanes]
                    mq = [queries * mask[k] for k in (0, 1)]
                    mg = [grads * mask[k] for k in (0, 1)]
                    return (
                        seg[:, rows].astype(F32),
                        [mq[k] + lterms[which, rows, :] * mask[1 - k] for k in (0, 1)],
                        [mg[k] + dterms[rows, :] * mask[1 - k] for k in (0, 1)],
                        jnp.concatenate(mq, axis=0),
                        jnp.concatenate(mg, axis=0),
                        [lt[which, 2 * p + k, :, rows] for k in (0, 1)],
                    )

                def products(unit):
                    b, c = unit
                    if b not in made:
                        made[b] = operands(b)
                    _, with_logs, with_sums, _, _, _ = made[b]
                    part = slice(c * kc, (c + 1) * kc)
                    keys, values = proj[1][part, lanes], proj[2][part, lanes]
                    return [
                        (
                            nt(keys * mask[k] + ones_at[k], with_logs[k]),
                            nt(values * mask[k] + ones_at[k], with_sums[k]),
                        )
                        for k in (0, 1)
                    ]

                ahead = products(units[0])
                for n, (b, c) in enumerate(units):
                    now = ahead
                    if n + 1 < len(units):
                        ahead = products(units[n + 1])
                    ids, _, _, mq, mg, fills = made[b]
                    if c == 0:
                        parts = [jnp.zeros((64, kb), F32)] * 2
                    part = slice(c * kc, (c + 1) * kc)
                    same = wide(scol[part, :], kb) == ids
                    shares, score_grads = [], []
                    for head in (0, 1):
                        scores, inner = now[head]
                        share = jnp.exp2(jnp.where(same, scores, fills[head]))
                        shares.append(share.astype(LOW))
                        score_grads.append((share * inner).astype(LOW))
                        krows = pl.ds(pl.multiple_of(p * 128 + head * 64, 64), 64)
                        parts[head] = parts[head] + nn(kt[krows, part], score_grads[head])
                    acc_k[part, :] += nn(jnp.concatenate(score_grads, axis=1), mq)
                    acc_v[part, :] += nn(jnp.concatenate(shares, axis=1), mg)
                    if c + 1 == tokens // kc:
                        turned = (jnp.concatenate(parts, axis=0) * 0.125).T
                        dq[rows_of(2 * i + b, kb), :] = turned.astype(LOW)

                @pl.when(i == 0)
                def _():
                    hook(p)

            loop(tokens // kb // 2, stretch)
            dk[...] = (acc_k[...] * (1.0 / LOG2_E)).astype(LOW)
            dv[...] = acc_v[...].astype(LOW)
            after(p, lanes, dq, dk, dv)
        loop(pairs, pair)

    def bias_sums(first, lanes, dq, dv):
        vacc[first : first + 1, lanes] = colsum(dq[...])
        vacc[first + 1 : first + 2, lanes] = colsum(dv[...])

    def cross_places(p):
        lanes = lanes_of(p)
        return z.at[:, lanes], h2.at[:, lanes], df.at[:, lanes]

    def self_places(p):
        return tuple(z.at[:, pl.ds(pl.multiple_of(p * third + k * 128, 128), 128)] for k in range(3))

    def cross_ready(i):
        rows = rows_of(i, wide_bt)
        before_attention(proj_c, 4, rows, da[rows, :])
        xt[:, rows] = h1[rows, :].T
        et[:, rows] = e[rows, :].T

    loop(wide_blocks, cross_ready)
    run_steps(("2e1", "2e2", "2e3", "2vo",))

    def cross_after(p, lanes, dq, dk, dv):
        bias_sums(9, lanes, dq, dv)
        both = jnp.concatenate([dk[...], dv[...]], axis=1)
        grads = jnp.concatenate([nn(xt[...], dq[...]), nn(et[...], both)], axis=1)
        gcr[p] = grads.astype(LOW).reshape(spots, 2, r, third)
        run_table([("1x0", "3c0", "3c1",), ("1x1", "3e0", "3e1", "4c0", "4c1",), ("1x2", "3e2", "3e3", "3vo", "5c0", "5c1",), ("1x3", "3x1", "4e2", "4e3", "4vo",)], p)

    def cross_mid(p):
        run_table([(), ("2x0", "3c2", "3c3",), ("2x1", "4c2", "4c3",), ("2x2", "3x0", "4e0", "4e1", "5c2", "5c3",)], p)

    attend_back(proj_c, 1, cross_places, cross_mid, cross_after)
    out_copy.wait()

    def after_cross(i):
        rows = rows_of(i)
        grad = dr[rows, :] + nt(z[rows, 0:width], att_w(4))
        xh = xh1[rows, :]
        add_row(1, colsum(grad))
        add_row(0, colsum(grad * xh))
        grad = norm_back(grad * vec[0:1, :], xh, rs1[rows, :])
        dr[rows, :] = grad
        low = grad.astype(LOW)
        da[rows, :] = low
        add_row(8, colsum(low))
        before_attention(proj_s, 0, rows, low)
        xt[:, rows] = x[rows, :].T

    loop(blocks, after_cross)

    gwo[...] = tn(proj_s[3][...], da[...]).astype(LOW).reshape(spots, 2, r, width)
    run_steps(("1wo", "2x3", "3x2", "4x0", "5e",))

    def pack_vectors():
        low = vacc[...].astype(LOW)
        row_id = lax.broadcasted_iota(jnp.int32, (width, 128), 0)
        lane_id = lax.broadcasted_iota(jnp.int32, (width, 128), 1)
        for d in range(nd):
            pick = jnp.where(
                (row_id == lane_id + d * own_width) & (lane_id < own_width), 1.0, 0.0
            ).astype(LOW)
            gve[d // 2, d % 2] = nn(low, pick).astype(LOW)

    def put(first, total):
        h1[first * r : first * r + total.shape[0], :] = total

    def self_after(p, lanes, dq, dk, dv):
        bias_sums(6, lanes, dq, dv)
        gse[p] = nn(xt[...], z[:, third_of(p)]).astype(LOW).reshape(spots, 2, r, third)
        run_table([("1s0", "3x3", "4x2", "5x0",), ("1s1", "3s0", "4x3", "5x2",), ("1s2", "3s1", "5x3", "5wo",), ("1s3", "3s2", "5s1",)], p)

    def self_mid(p):
        run_table([("2wo", "4x1", "5vo",), ("2s0", "3wo", "5x1",), ("2s1", "4wo", "4s0",), ("2s2", "4s1", "5s0",)], p)

        @pl.when(p == pairs - 1)
        def _():
            for j in range(chunks):
                put(8 + j, final_step(grps["c", j]))
                put(12 + j, final_step(grps["e", j]))
            put(7, final_step(grps["vo", 0]))

    attend_back(proj_s, 0, self_places, self_mid, self_after)
    pack_vectors()
    run_steps(("1v",))

    def encoder_out(i):
        rows = pl.ds(i * wide_bt, wide_bt)
        e[rows, :] = (nt(h2[rows, :], att_w(5)) + nt(df[rows, :], att_w(6))).astype(LOW)
        copy(4 + i, e.at[rows, :], eg_h.at[rows, :]).start()

    def input_out(i):
        rows = pl.ds(i * wide_bt, wide_bt)
        da[rows, :] = (
            dr[rows, :] + nt(z[rows, 0 : 3 * width], wself[...].reshape(width, 3 * width))
        ).astype(LOW)

    last_pair = grps["s", pairs - 1]

    def put_pair(name, base, i, total=None):
        total = final_step(grps[name, i]) if total is None else total.astype(LOW)
        for k in range(3):
            h1[(base + k) * r : (base + k + 1) * r, i * 128 : (i + 1) * 128] = total[:, k * 128 : (k + 1) * 128]

    encoder_out(0)
    run_steps(("2v", "2s3", "4s2"))
    encoder_out(1)
    third_direct(last_pair, zs, 0)
    third_direct(grps["v", 0], zv, 1)
    run_steps(("5s2",))
    input_out(0)
    put(3, final_step(grps["wo", 0]))
    for i in range(pairs):
        put_pair("x", 4, i)
    input_out(1)
    ig_copy = copy(0, da, ig_h)
    ig_copy.start()
    for i in range(pairs - 1):
        put_pair("s", 0, i)
    gvec[...] = final_direct(zv, 1)
    put_pair("s", 0, pairs - 1, final_direct(zs, 0))

    stores = [
        copy(1, h1.at[pl.ds(0, 8 * r), :], ga_h),
        copy(3, h1.at[pl.ds(8 * r, 4 * r), :], gc_h),
    ] + [
        copy(8 + j, h1.at[pl.ds((12 + j) * r, r), :], ge_h.at[:, pl.ds(j * width, width)])
        for j in range(chunks)
    ]
    for c in stores:
        c.start()

    def square(values):
        return fold(values * values, jnp.add)

    squares = lax.fori_loop(
        0, 16, lambda i, had: had + square(h1[rows_of(i, r), :].astype(F32)), jnp.zeros((8, width), F32)
    )
    total = jnp.sum(jnp.sum(squares, axis=0, keepdims=True), axis=1, keepdims=True) + jnp.sum(
        jnp.sum(square(gvec[...]), axis=0, keepdims=True), axis=1, keepdims=True
    )
    nall[me] = jnp.broadcast_to(total, (8, 128))
    for peer in dp_peers:
        remote(nall.at[me], nall.at[me], norm_sems.at[0], norm_sems.at[1], peer).start()
    siblings = pl.ds(0, nd - 1)
    wait_bytes(nall.at[siblings], norm_sems.at[1])
    whole = nall[0]
    for q in range(1, nd):
        whole = whole + nall[q]
    norm[...] = jnp.sqrt(whole)
    wait_bytes(nall.at[siblings], norm_sems.at[0])

    finish_direct(grps.pop(("s", pairs - 1)), zs, 0)
    finish_direct(grps.pop(("v", 0)), zv, 1)
    for g in grps.values():
        finish_sends(g)
    for c in stores:
        c.wait()
    for i in range(wide_blocks):
        rows = pl.ds(i * wide_bt, wide_bt)
        copy(4 + i, e.at[rows, :], eg_h.at[rows, :]).wait()
    ig_copy.wait()


def run_step(nd, nr, seg, ham, pri, vec_w, dec, tgt, enc, cot, aw, ew, cw):
    tokens, width = dec.shape
    hidden = ew.shape[1]
    spots, r = nd // 2, width // nd
    count = 2 * (hidden // width) + 3 + 2 * (width // 128)
    pairs = width // 128
    any_spec = pl.BlockSpec(memory_space=pl.ANY)
    vmem = pl.BlockSpec(memory_space=pltpu.VMEM)
    low = functools.partial(pltpu.VMEM, dtype=LOW)
    full = functools.partial(pltpu.VMEM, dtype=F32)
    vr = (vec_w.shape[0] + 15) // 16 * 16
    dma = pltpu.SemaphoreType.DMA
    return pl.pallas_call(
        functools.partial(step_kernel, nd, nr),
        out_shape=(
            jax.ShapeDtypeStruct((tokens, width), LOW),
            jax.ShapeDtypeStruct((tokens, width), LOW),
            jax.ShapeDtypeStruct((tokens, width), LOW),
            jax.ShapeDtypeStruct((8 * r, width), LOW),
            jax.ShapeDtypeStruct((r, hidden), LOW),
            jax.ShapeDtypeStruct((4 * r, width), LOW),
            jax.ShapeDtypeStruct((vr, 128), F32),
            jax.ShapeDtypeStruct((8, 128), F32),
        ),
        in_specs=[vmem] * 4 + [any_spec] * 7,
        out_specs=[any_spec] * 6 + [vmem] * 2,
        scratch_shapes=[
            low((spots, 2, r, 3 * width)), low((5, spots, 2, r, width)), low((spots, 2, r, hidden)), low((spots, 2, 4 * r, width)),
            low((tokens, width)), low((tokens, width)),
            *[low((tokens, width)) for _ in range(8)],
            full((tokens, width)), full((tokens, 1)),
            low((tokens, width)), low((tokens, width)),
            low((tokens, hidden)), low((tokens, hidden)),
            low((tokens, width)), full((tokens, width)), low((tokens, width)),
            low((tokens, width)), low((width, tokens)),
            full((tokens, 128)), full((tokens, 128)),
            full((2, H, 1, tokens)), low((2, tokens, 128)), low((tokens, 128)),
            full((vr, width)), full((vr, width)),
            low((256, hidden)), full((tokens, 128)), full((tokens, 128)),
            full((8, 128)),
            low((spots, 2, r, hidden)), low((spots, 2, 4 * r, width)),
            low((pairs, spots, 2, r, 384)), low((pairs, spots, 2, r, 384)),
            low((spots, 2, r, width)), low((spots, 2, r, width)), low((spots, 2, vr, 128)),
            low((2 * pairs, spots, r, 384)), low((2 * pairs, spots - 1, r, 384)), low((2 * pairs, 2, r, 384)),
            low((2, spots, r, width)), low((2, spots - 1, r, width)), low((2, 2, r, width)),
            low((spots, vr, 128)), low((spots - 1, vr, 128)), low((2, vr, 128)),
            low((r, hidden)), low((4 * r, width)), low((nr, r, 384)), low((nr, vr, 128)),
            low((spots, 2, vr, 128)), full((nd, 8, 128)),
            dma((8 + hidden // width,)), dma((6, 5 + pairs)), dma((10, count)), dma((2, 2)), dma((2,)),
            pltpu.SemaphoreType.REGULAR,
        ],
        compiler_params=pltpu.CompilerParams(
            vmem_limit_bytes=64 * MIB - 64 * 1024, collective_id=0, has_side_effects=True
        ),
        cost_estimate=pl.CostEstimate(flops=41 * 10**9, bytes_accessed=30 * MIB, transcendentals=50 * 10**6),
        name="layer_step",
    )(seg, ham, pri, vec_w, dec, tgt, enc, cot, aw, ew, cw)


def adamw_kernel(*args):
    norm, args = args[0], args[1:]
    moved_in, raws, states = args[0:3], args[3:7], args[7:19]
    moved_out, outs, norm_out = args[19:22], args[22:38], args[38]
    bufs, sems = args[39:-1], args[-1]
    moved_a, moved_b, held, made = bufs[0:3], bufs[3:6], bufs[6:22], bufs[22:38]
    pending = []

    def copy(source, dest):
        c = pltpu.make_async_copy(source, dest, sems.at[len(pending)])
        pending.append(c)
        c.start()
        return c

    fetched = []
    for i in range(4):
        sources = (raws[i],) + states[3 * i : 3 * i + 3]
        fetched.append([copy(a, b) for a, b in zip(sources, held[4 * i : 4 * i + 4])])
    moves = [copy(a, b) for a, b in zip(moved_in, moved_a)]
    factor = CLIP_NORM / jnp.maximum(norm[0:1, 0:1], CLIP_NORM)
    norm_out[...] = norm[0:1, 0:1]
    stores = []
    for i in range(4):
        for c in fetched[i]:
            c.wait()
        raw, weight, first, second = (ref[...] for ref in held[4 * i : 4 * i + 4])
        rate = RATE_VECTOR if i == 3 else RATE_MATRIX
        clipped = raw[0 : weight.shape[0], 0 : weight.shape[1]].astype(F32) * factor
        first_new = BETA_ONE * first + (1.0 - BETA_ONE) * clipped
        second_new = BETA_TWO * second + (1.0 - BETA_TWO) * clipped * clipped
        first_hat = first_new / (1.0 - BETA_ONE**STEP)
        second_hat = second_new / (1.0 - BETA_TWO**STEP)
        weight_new = weight - rate * (
            first_hat / (jnp.sqrt(second_hat) + ADAM_EPS) + WEIGHT_DECAY * weight
        )
        for k, value in enumerate((clipped, first_new, second_new, weight_new)):
            made[4 * i + k][...] = value
            stores.append(copy(made[4 * i + k], outs[4 * i + k]))
    for k in range(3):
        moves[k].wait()
        if moved_a[k].dtype == moved_b[k].dtype:
            stores.append(copy(moved_a[k], moved_out[k]))
        else:
            moved_b[k][...] = moved_a[k][...].astype(moved_b[k].dtype)
            stores.append(copy(moved_b[k], moved_out[k]))
    for c in stores:
        c.wait()


def run_adamw(norm, moved, raws, states):
    any_spec = pl.BlockSpec(memory_space=pl.ANY)
    vmem = pl.BlockSpec(memory_space=pltpu.VMEM)
    flat = [a for state in states for a in state]
    moved_types = (LOW, F32, F32)
    made = [state[0].shape for state in states for _ in range(4)]
    held = [a for raw, state in zip(raws, states) for a in (raw,) + tuple(state)]
    scratch = [pltpu.VMEM(a.shape, a.dtype) for a in moved]
    scratch += [pltpu.VMEM(a.shape if d == F32 else (16, 128), d) for a, d in zip(moved, moved_types)]
    scratch += [pltpu.VMEM(a.shape, a.dtype) for a in held] + [pltpu.VMEM(m, F32) for m in made]
    outs = pl.pallas_call(
        adamw_kernel,
        in_specs=[vmem] + [any_spec] * 19,
        out_specs=[any_spec] * 19 + [vmem],
        out_shape=[jax.ShapeDtypeStruct(a.shape, d) for a, d in zip(moved, moved_types)]
        + [jax.ShapeDtypeStruct(m, F32) for m in made]
        + [jax.ShapeDtypeStruct((1, 1), F32)],
        scratch_shapes=scratch + [pltpu.SemaphoreType.DMA((38,))],
        compiler_params=pltpu.CompilerParams(vmem_limit_bytes=64 * MIB - 64 * 1024),
        cost_estimate=pl.CostEstimate(flops=10**7, bytes_accessed=21 * MIB, transcendentals=10**6),
        name="adamw",
    )(norm, *moved, *raws, *flat)
    return outs[3:19], outs[0:3], outs[19]


def per_device(
    nd,
    nr,
    decoder_input,
    target_embedding,
    encoder_states,
    cotangent,
    segments,
    hamming,
    priority,
    attention_weight,
    attention_first,
    attention_second,
    expand_weight,
    expand_first,
    expand_second,
    contract_weight,
    contract_first,
    contract_second,
    vector_weight,
    vector_first,
    vector_second,
):
    width = decoder_input.shape[1]
    attention = tuple(
        a.reshape(-1, width) for a in (attention_weight, attention_first, attention_second)
    )
    expand = (expand_weight, expand_first, expand_second)
    contract = (contract_weight, contract_first, contract_second)
    vector = (vector_weight, vector_first, vector_second)
    layer_output, input_grad, encoder_grad, ga, ge, gc, gv, norm = run_step(
        nd, nr, segments, hamming, priority, vector_weight, decoder_input, target_embedding,
        encoder_states, cotangent, attention[0], expand_weight, contract_weight,
    )
    outs, moved, whole_norm = run_adamw(
        norm, (layer_output, input_grad, encoder_grad), (ga, ge, gc, gv), (attention, expand, contract, vector)
    )
    attention_outs = tuple(a.reshape(attention_weight.shape) for a in outs[0:4])
    return tuple(moved) + attention_outs + tuple(outs[4:16]) + (whole_norm.reshape(()),)


def solution(mesh):
    rows = P(("rep", "dp"), None)
    owned = (P(None, "dp", None),) * 3 + (P("dp", None),) * 6 + (P(None, "dp"),) * 3
    made = (P(None, "dp", None),) * 4 + (P("dp", None),) * 8 + (P(None, "dp"),) * 4
    return jax.shard_map(
        functools.partial(per_device, mesh.shape["dp"], mesh.shape["rep"]),
        mesh=mesh,
        in_specs=(rows,) * 7 + owned,
        out_specs=(rows,) * 3 + made + (P(),),
        check_vma=False,
    )
```

time: 588 us -> 174 us (0.30)
  matrix products: 246 us -> 0 us
  Pallas kernels: 0 us -> 173 us
  waiting for transfers between devices: 141 us -> 0 us
  other arithmetic: 108 us -> 0 us
  blocking collectives: 37 us -> 0 us
  local copies, waits for them, and re-layouts: 30.9 us -> 0 us
  between operations: 20.5 us -> 0.85 us
    dot_general x54 -> x0, matrix products: 246 us -> none  [the longest x4 44.5 us: attend_back(): jnp.einsum('qhd,khd->hqk', grad_block, value_rows, preferred_element_type...]
    pallas_call x0 -> x2, Pallas kernels: none -> 173 us  [the longest x1 164 us: run_step(): pl.pallas_call(functools.partial(step_kernel, nd, nr), out_shape=(jax.Sha...]
    reduce_scatter x3 -> x0, waiting for transfers between devices: 60.6 us -> none  [the longest x1 54.6 us: per_device(): lax.psum_scatter(summed[0].astype(jnp.bfloat16), 'dp', scatter_dimension=...]
    convert_element_type x9 -> x0, other arithmetic: 52.2 us -> none  [the longest x4 45.8 us: attend_back(): score_grad = (shares * (share_grad - inner)).astype(jnp.bfloat16)]
    psum x1 -> x0, waiting for transfers between devices: 41.8 us -> none  [per_device(): lax.psum(attention_raw.astype(jnp.bfloat16), 'rep').astype(jnp.float32)]
    reduce_sum x21 -> x0, other arithmetic: 40.9 us -> none  [the longest x4 24.4 us: attend_row(): totals = jnp.sum(raised, axis=2, keepdims=True)]
    unnamed x283 -> x0, local copies, waits for them, and re-layouts: 29.4 us -> none
    psum x2 -> x0, blocking collectives: 26.4 us -> none  [the longest x1 14.4 us: per_device(): total_square = lax.psum(local_square, 'dp')]
  transfers between devices with their start and end apart: 8 -> 0, of which waited for: 5 -> 0; matrix products, arithmetic and copies ran while one was open for 34% -> 0% of each run, Pallas kernels for 0% -> 0%
where the time goes in v1:
time: 174 us
  Pallas kernels  173 us (99%)
    pallas_call x1, Pallas kernels, run_step(): pl.pallas_call(functools.partial(step_kernel, nd, nr), out_shape=(jax.Sha...  164 us
    pallas_call x1, Pallas kernels, run_adamw(): pl.pallas_call(adamw_kernel, in_specs=[vmem] + [any_spec] * 19, out_specs...  9.18 us

profile of v1, /device:TPU:0, one launch (start us, length us, event | category | flops | bytes accessed | tf_op | source)
XLA Modules:
  0.0 174.2 jit_solution(8671818398751314836)
XLA Ops:
  0.7 164.1 %layer_step.1 = (bf16[1024,512]{1,0:T(8,128)(2,1)}, bf16[1024,512]{1,0:T(8,128)(2,1)}, bf16[1024,512]{1,0:T(8,128)(2,1)}, bf16[512,512]{1,0:T(8,128)(2,1)}, bf16...) custom-call(s32[1,1024]{1,0:T(1,128)} %seg.1, s32[1,51]{1,0:T(1,128)} %ham.1, ...), custom_call_target="tpu_custom_call" | custom-call | flops 41000001536 | bytes 31457280 | tf_op jit(solution)/shard_map/layer_step/pallas_call | solution.py:950
  164.8 9.2 %adamw.1 = (bf16[1024,512]{1,0:T(8,128)(2,1)}, f32[1024,512]{1,0:T(8,128)}, f32[1024,512]{1,0:T(8,128)}, f32[512,512]{1,0:T(8,128)}, f32[512,512]{1,0:T(8,128)},...) custom-call(f32[8,128]{1,0:T(8,128)} %get-tuple-element.48.args_0_, ...), custom_call_target="tpu_custom_call" | custom-call | flops 10000000 | bytes 22020096 | tf_op jit(solution)/shard_map/adamw/pallas_call | solution.py:1056
